TPU v7x, 512 devices: a whole 4x8x8 slice. The times are simulated.
512 devices in a mesh: dp: 32 (over x_hi, z, core), tensor: 16 (over x_lo, y).
Axes of the slice: x: 4 (x_hi: 2, x_lo: 2; x = x_hi * 2 + x_lo), y: 8, z: 8, core: 2. Of those that a mesh axis runs over, the one named last changes fastest.
Arguments:
- weight: bfloat16 [7168, 18432], P('dp', 'tensor'), may hold values from -0.015625 to 0.015625
- gradient: bfloat16 [7168, 18432], P('dp', 'tensor'), may hold values from -6 to 6
- momentum: float32 [7168, 18432], P('dp', 'tensor'), may hold values from -6 to 6
- basis: float32 [7168, 512], P('dp'), may hold values from -0.0625 to 0.0625
Outputs:
- new_momentum: float32 [7168, 18432], P('dp', 'tensor')
- new_basis: float32 [7168, 512], P('dp')
- row_values: bfloat16 [18432, 7168], P(('tensor', 'dp'))
- row_scales: float32 [18432, 56], P(('tensor', 'dp'))
- column_values: bfloat16 [7168, 18432], P(('dp', 'tensor'))
- column_scales: float32 [7168, 144], P(('dp', 'tensor'))
All inputs are finite; a program needn't handle non-finite values. Where the computation divides by a largest or mean magnitude, that divisor is 1e-20 or more.
Results may differ from a plain program's by a relative error of at most 0.0056.
Values may be sent and summed in bfloat16 or wider, within the bound.
A program may use at most 64 MiB of HBM per device.

v0:
```python
import math

import jax
import jax.numpy as jnp
from jax import lax
from jax.sharding import PartitionSpec as P

D = 7168
FF = 18432
TILE = 128


decay_rate = 0.95
step_size = 0.3
epsilon = 1e-06


def quantize(block):
    rows = block.shape[0]
    width = block.shape[1]
    tiles = block.astype(jnp.float32).reshape(rows, width // TILE, TILE)
    largest = jnp.max(jnp.abs(tiles), axis=2)
    values = (tiles / (largest[:, :, None] + epsilon)).astype(jnp.bfloat16)
    return (values.reshape(rows, width), largest)


def orthonormal(proj, gram):
    lower = jnp.linalg.cholesky(gram)
    return jax.scipy.linalg.solve_triangular(lower, proj.T, lower=True).T


def on_device(weight, gradient, momentum, basis):
    highest = lax.Precision.HIGHEST
    buffer = momentum + gradient.astype(jnp.float32)
    proj = lax.psum(jnp.dot(buffer.T, basis, precision=highest), "dp")
    gram = lax.psum(jnp.dot(proj.T, proj, precision=highest), "tensor")
    ortho = orthonormal(proj, gram)
    back = lax.psum(jnp.dot(buffer, ortho, precision=highest), "tensor")
    colsq = lax.psum(jnp.sum(back * back, axis=0), "dp")
    new_basis = back / jnp.sqrt(colsq + epsilon)
    new_momentum = buffer - (1.0 - decay_rate) * jnp.dot(back, ortho.T, precision=highest)
    factor = step_size * math.sqrt(FF / D)
    updated = (
        weight.astype(jnp.float32) - factor * jnp.dot(new_basis, ortho.T, precision=highest)
    ).astype(jnp.bfloat16)
    full_rows = lax.all_to_all(updated.T, "dp", split_axis=0, concat_axis=1, tiled=True)
    row_values, row_scales = quantize(full_rows)
    full_columns = lax.all_to_all(updated, "tensor", split_axis=0, concat_axis=1, tiled=True)
    column_values, column_scales = quantize(full_columns)
    return (new_momentum, new_basis, row_values, row_scales, column_values, column_scales)


def solution(mesh):
    placed = (P("dp", "tensor"), P("dp", "tensor"), P("dp", "tensor"), P("dp", None))
    return jax.shard_map(
        on_device,
        mesh=mesh,
        in_specs=placed,
        out_specs=(
            P("dp", "tensor"),
            P("dp", None),
            P(("tensor", "dp"), None),
            P(("tensor", "dp"), None),
            P(("dp", "tensor"), None),
            P(("dp", "tensor"), None),
        ),
        check_vma=False,
    )
```

profile of v0, /device:TPU:1, one launch (start us, length us, event | category | flops | bytes accessed | tf_op | source)
XLA Modules:
  0.0 881.8 jit_solution(6630755391166886870)
XLA Ops:
  8.2 4.9 fusion.17
  13.1 284.7 %all-reduce.5.cloned.1.call-done = f32[1152,512]{1,0:T(8,128)} async-done(((f32[1152,512]{1,0:T(8,128)}), f32[1152,512]{1,0:T(8,128)}) %all-reduce.5.cloned.1.call-update) | async-done | bytes 2359312 | tf_op jit(solution)/shard_map/psum | solution.py:35
  297.9 7.7 fusion.41
  305.8 130.4 %all-reduce.7.cloned.1.call-done = f32[512,512]{0,1:T(8,128)} async-done(((f32[512,512]{0,1:T(8,128)}), f32[512,512]{0,1:T(8,128)}) %all-reduce.7.cloned.1.call-update) | async-done | bytes 1048592 | tf_op jit(solution)/shard_map/psum | solution.py:36
  439.1 11.7 %cholesky.104 = f32[128,128]{1,0:T(8,128)S(1)} custom-call(f32[128,128]{1,0:T(8,128)S(1)} %cholesky.266), custom_call_target="Cholesky" | custom-call | tf_op jit(solution)/shard_map/jit(cholesky)/cholesky | solution.py:28
  452.0 9.8 %custom-call.31 = f32[1,128,128]{1,2,0:T(8,128)S(1)} custom-call(f32[1,128,128]{2,1,0:T(8,128)S(1)} %get-tuple-element.33), custom_call_target="InvertDiagBlocksLowerTriangular" | custom-call | tf_op jit(solution)/shard_map/jit(cholesky)/cholesky | solution.py:28
  461.8 1.9 constant_dynamic-update-slice_fusion.3
  465.0 11.7 %cholesky.217 = f32[128,128]{1,0:T(8,128)S(1)} custom-call(f32[128,128]{1,0:T(8,128)S(1)} %cholesky.270), custom_call_target="Cholesky" | custom-call | tf_op jit(solution)/shard_map/jit(cholesky)/cholesky | solution.py:28
  477.4 10.2 %custom-call.32 = f32[1,128,128]{1,2,0:T(8,128)S(1)} custom-call(f32[1,128,128]{2,1,0:T(8,128)S(1)} %get-tuple-element.30), custom_call_target="InvertDiagBlocksLowerTriangular" | custom-call | tf_op jit(solution)/shard_map/jit(cholesky)/cholesky | solution.py:28
  490.1 11.7 %cholesky.238 = f32[128,128]{1,0:T(8,128)S(1)} custom-call(f32[128,128]{1,0:T(8,128)S(1)} %cholesky.275), custom_call_target="Cholesky" | custom-call | tf_op jit(solution)/shard_map/jit(cholesky)/cholesky | solution.py:28
  502.5 9.8 %custom-call.33 = f32[1,128,128]{1,2,0:T(8,128)S(1)} custom-call(f32[1,128,128]{2,1,0:T(8,128)S(1)} %get-tuple-element.27), custom_call_target="InvertDiagBlocksLowerTriangular" | custom-call | tf_op jit(solution)/shard_map/jit(cholesky)/cholesky | solution.py:28
  514.5 11.7 %cholesky.255 = f32[128,128]{1,0:T(8,128)S(1)} custom-call(f32[128,128]{1,0:T(8,128)S(1)} %convolution_subtract_fusion.5), custom_call_target="Cholesky" | custom-call | tf_op jit(solution)/shard_map/jit(cholesky)/cholesky | solution.py:28
  531.4 2.5 select_select_fusion
  533.9 11.6 %while.1 = (s32[]{:T(128)}, f32[512,512]{1,0:T(8,128)}, s32[4,2]{0,1:T(2,128)S(1)}, f32[4,128,128]{2,1,0:T(8,128)S(1)}, s32[]{:T(128)}) while((s32[]{:T(128)}, f32[512,512]{1,0:T(8,128)}, s32[4,2]{0,1:T(2,128)S(1)}, f32[4,128,128]{2,1,0:T(8,128)S(1)}, s32[]{:T(128)}) %tuple.31), condition=%wide.while_cond, body=%wide.while_body.sunk | while | flops 2 | bytes 131189 | solution.py:29
  534.5 2.3 bitcast_dynamic-update-slice_fusion.2
  537.4 2.3 bitcast_dynamic-update-slice_fusion.2
  540.3 2.3 bitcast_dynamic-update-slice_fusion.2
  543.2 2.2 bitcast_dynamic-update-slice_fusion.2
  545.4 39.9 %custom-call.34 = f32[4,128,128]{1,2,0:T(8,128)} custom-call(f32[4,128,128]{2,1,0:T(8,128)S(1)} %get-tuple-element.13), custom_call_target="InvertDiagBlocksLowerTriangular" | custom-call | tf_op jit(solution)/shard_map/jit(_solve_triangular)/triangular_solve | solution.py:29
  589.7 3.1 convolution_subtract_fusion.1
  593.6 4.3 convolution_subtract_fusion
  598.7 3.3 fusion.16
  602.1 138.0 %all-reduce.9.cloned.1.call-done = f32[224,512]{1,0:T(8,128)} async-done(((f32[224,512]{1,0:T(8,128)}), f32[224,512]{1,0:T(8,128)}) %all-reduce.9.cloned.1.call-update) | async-done | bytes 458768 | tf_op jit(solution)/shard_map/psum | solution.py:38
  741.1 76.1 %psum.31 = f32[512]{0:T(512)S(1)} all-reduce(f32[512]{0:T(512)S(1)} %multiply_reduce_fusion), channel_id=1, replica_groups=mesh['dp'=32,'tensor'=16] {'dp'}, use_global_device_ids=true, to_apply=%region_12.13 | all-reduce | flops 512 | bytes 4096 | tf_op jit(solution)/shard_map/psum | solution.py:39
  818.4 3.5 fusion.2
  822.8 3.6 all-to-all-start.1
  827.7 4.9 fusion.1
  832.6 10.3 %all-to-all-done.1 = bf16[16,14,1152]{2,1,0:T(8,128)(2,1)S(1)} async-done(((bf16[16,14,1152]{2,1,0:T(8,128)(2,1)}), bf16[16,14,1152]{2,1,0:T(8,128)(2,1)S(1)}, u32[]{:S(2)}, u32[]{:S(2)}) %all-to-all-start.1) | async-done | bytes 516128 | tf_op jit(solution)/shard_map/all_to_all | solution.py:48
  842.9 4.5 all-to-all-start
  849.7 2.3 abs.23
  855.6 12.4 %all-to-all-done = bf16[32,36,224]{2,1,0:T(8,128)(2,1)S(1)} async-done(((bf16[32,36,224]{2,1,0:T(8,128)(2,1)}), bf16[32,36,224]{2,1,0:T(8,128)(2,1)S(1)}, u32[]{:S(2)}, u32[]{:S(2)}) %all-to-all-start) | async-done | bytes 516128 | tf_op jit(solution)/shard_map/all_to_all | solution.py:46
  869.9 2.0 abs.20
  (99 shorter events, 38.6 us)
Async XLA Ops:
  7.2 1.0 copy-start
  7.2 290.7 %all-reduce.5.cloned.1.call-start = ((), (), s32[]{:S(2)}) async-start(), calls=%async_computation.2 | async-start | bytes 4718592 | tf_op jit(solution)/shard_map/psum | solution.py:35
  13.1 423.1 %all-reduce.7.cloned.1.call-start = ((), (), s32[]{:S(2)}) async-start(), calls=%async_computation.3 | async-start | bytes 2097152 | tf_op jit(solution)/shard_map/psum | solution.py:36
  305.6 434.5 %all-reduce.9.cloned.1.call-start = ((), (), s32[]{:S(2)}) async-start(), calls=%async_computation.4 | async-start | bytes 917504 | tf_op jit(solution)/shard_map/psum | solution.py:38
  436.2 1.7 copy-start.4
  438.1 1.0 copy-start.5
  488.5 96.9 %copy-start.1 = (f32[1152,512]{1,0:T(8,128)S(1)}, f32[1152,512]{1,0:T(8,128)}, u32[]{:S(2)}) copy-start(f32[1152,512]{1,0:T(8,128)} %all-reduce.5.cloned.1.call-done) | copy-start | bytes 7077892
  585.4 3.6 copy-start.11
  589.7 8.9 %copy-start.2 = (f32[128,1152]{1,0:T(8,128)}, f32[128,1152]{1,0:T(8,128)S(1)}, u32[]{:S(2)}) copy-start(f32[128,1152]{1,0:T(8,128)S(1)} %fusion.29) | copy-start | bytes 1769476
  593.6 5.1 copy-start.6
  593.6 5.1 copy-start.7
  593.6 5.1 copy-start.9
  598.7 219.7 %copy-start.8 = (f32[128,1152]{1,0:T(8,128)}, f32[128,1152]{1,0:T(8,128)S(1)}, u32[]{:S(2)}) copy-start(f32[128,1152]{1,0:T(8,128)S(1)} %fusion.26) | copy-start | bytes 1769476
  598.7 219.7 %copy-start.14 = (bf16[224,1152]{1,0:T(8,128)(2,1)S(1)}, bf16[224,1152]{1,0:T(8,128)(2,1)}, u32[]{:S(2)}) copy-start(bf16[224,1152]{1,0:T(8,128)(2,1)} %param.4) | copy-start | bytes 1548292
  818.4 3.5 copy-start.10
  821.9 5.8 copy-start.3
  822.8 20.0 %all-to-all-start.1 = ((bf16[16,14,1152]{2,1,0:T(8,128)(2,1)}), bf16[16,14,1152]{2,1,0:T(8,128)(2,1)S(1)}, u32[]{:S(2)}, u32[]{:S(2)}) async-start(bf16[16,14,1152]{2,1,0:T(8,128)(2,1)} %all_to_all.22), calls=%async_computation.1 | async-start | bytes 1179648 | tf_op jit(solution)/shard_map/all_to_all | solution.py:48
  842.9 25.2 %all-to-all-start = ((bf16[32,36,224]{2,1,0:T(8,128)(2,1)}), bf16[32,36,224]{2,1,0:T(8,128)(2,1)S(1)}, u32[]{:S(2)}, u32[]{:S(2)}) async-start(bf16[32,36,224]{2,1,0:T(8,128)(2,1)} %all_to_all.20), calls=%async_computation | async-start | bytes 1310720 | tf_op jit(solution)/shard_map/all_to_all | solution.py:46
  853.8 0.8 copy-start.13
  873.4 0.7 copy-start.12
Sparse Core Ops, SparseCore 0:
  13.2 284.6 all-reduce.4
  305.7 130.4 all-reduce.6
  602.2 137.8 all-reduce.8
where the time goes:
time: 889 us; the launch traced here: 882 us
  waiting for transfers between devices  576 us (65%)
  other arithmetic  131 us (15%)
  blocking collectives  76.1 us (9%)
  matrix products  45.4 us (5%)
  local copies, waits for them, and re-layouts  27.8 us (3%)
  between operations  17.1 us (2%)
    psum x1, waiting for transfers between devices, on_device(): proj = lax.psum(jnp.dot(buffer.T, basis, precision=highest), 'dp')  285 us
    psum x1, waiting for transfers between devices, on_device(): back = lax.psum(jnp.dot(buffer, ortho, precision=highest), 'tensor')  138 us
    psum x1, waiting for transfers between devices, on_device(): gram = lax.psum(jnp.dot(proj.T, proj, precision=highest), 'tensor')  130 us
    another operation x14, other arithmetic, orthonormal(): lower = jnp.linalg.cholesky(gram)  80.5 us
    psum x1, blocking collectives, on_device(): colsq = lax.psum(jnp.sum(back * back, axis=0), 'dp')  76.1 us
    another operation x3, other arithmetic, orthonormal(): return jax.scipy.linalg.solve_triangular(lower, proj.T, lower=True).T  42.4 us
  transfers between devices with their start and end apart: 5, of which 5 were waited for; matrix products, arithmetic and copies ran while one was open for 2% of the time, Pallas kernels for 0%

commit v1 on v0

v1 whole, which is shorter than its diff:
```python
import functools
import math

import jax
import jax.numpy as jnp
from jax import lax
from jax.experimental import pallas as pl
from jax.experimental.pallas import tpu as pltpu
from jax.sharding import PartitionSpec as P

RANK = 512
BLOCK = 128
STRIP = 8
HIGHEST = lax.Precision.HIGHEST


def dot_nt(a, b, precision=None):
    return lax.dot_general(a, b, (((1,), (1,)), ((), ())), precision=precision, preferred_element_type=jnp.float32)


def dot_nn(a, b, precision=None):
    return lax.dot_general(a, b, (((1,), (0,)), ((), ())), precision=precision, preferred_element_type=jnp.float32)


def invert_block(tiles):
    shape = (STRIP, BLOCK)
    count = BLOCK // STRIP
    row_of = lax.broadcasted_iota(jnp.int32, shape, 0)
    lane_of = lax.broadcasted_iota(jnp.int32, shape, 1)
    tiles = list(tiles)
    own = [jnp.where(lane_of == row_of + STRIP * i, 1.0, 0.0).astype(jnp.float32) for i in range(count)]
    for s in range(count):
        spread = lambda tile, m, lane: jnp.broadcast_to(tile[m:m + 1, lane:lane + 1], shape)
        small = [[spread(tiles[s], m, STRIP * s + k) for k in range(m + 1)] for m in range(STRIP)]
        rows = [jnp.broadcast_to(tiles[s][m:m + 1, :], shape) for m in range(STRIP)]
        extra = [jnp.broadcast_to(own[s][m:m + 1, :], shape) for m in range(STRIP)]
        factor = [[None] * STRIP for _ in range(STRIP)]
        inverse, root = [], []
        for k in range(STRIP):
            r = lax.rsqrt(small[k][k])
            root.append(r)
            inverse.append(r * r)
            for m in range(k + 1, STRIP):
                f = small[m][k] * inverse[k]
                factor[m][k] = f
                for j in range(k + 1, m + 1):
                    small[m][j] = small[m][j] - f * small[j][k]
                rows[m] = rows[m] - f * rows[k]
                extra[m] = extra[m] - f * extra[k]
        for i in range(s + 1, count):
            cols = [jnp.broadcast_to(tiles[i][:, STRIP * s + k:STRIP * s + k + 1], shape) for k in range(STRIP)]
            for k in range(STRIP):
                for m in range(k + 1, STRIP):
                    cols[m] = cols[m] - cols[k] * factor[m][k]
            for k in range(STRIP):
                g = cols[k] * inverse[k]
                tiles[i] = tiles[i] - g * rows[k]
                own[i] = own[i] - g * extra[k]
        done = extra[0] * root[0]
        for m in range(1, STRIP):
            done = jnp.where(row_of == m, extra[m] * root[m], done)
        own[s] = done
    return own


def cholesky_kernel(gram_ref, inv_ref, a_ref, small_ref):
    a_ref[...] = gram_ref[...]
    rank = gram_ref.shape[0]
    row_of = lax.broadcasted_iota(jnp.int32, (rank, rank), 0)
    inv_ref[...] = jnp.where(row_of == lax.broadcasted_iota(jnp.int32, (rank, rank), 1), 1.0, 0.0).astype(jnp.float32)

    def step(b, carry):
        at = pl.multiple_of(b * BLOCK, BLOCK)
        tiles = [a_ref[pl.ds(pl.multiple_of(at + STRIP * i, STRIP), STRIP), pl.ds(at, BLOCK)] for i in range(BLOCK // STRIP)]
        own = invert_block(tiles)
        for i, tile in enumerate(own):
            small_ref[pl.ds(STRIP * i, STRIP), :] = tile
        inverse = small_ref[...]
        rows = dot_nn(inverse, inv_ref[pl.ds(at, BLOCK), :], HIGHEST)
        below = lax.broadcasted_iota(jnp.int32, (rank, BLOCK), 0) >= at + BLOCK
        panel = jnp.where(below, dot_nt(a_ref[:, pl.ds(at, BLOCK)], inverse, HIGHEST), 0.0)
        inv_ref[pl.ds(at, BLOCK), :] = rows
        a_ref[...] -= dot_nt(panel, panel, HIGHEST)
        inv_ref[...] -= dot_nn(panel, rows, HIGHEST)
        return carry

    lax.fori_loop(0, rank // BLOCK, step, 0)


def inverse_factor(gram):
    return pl.pallas_call(
        cholesky_kernel,
        out_shape=jax.ShapeDtypeStruct(gram.shape, jnp.float32),
        in_specs=[pl.BlockSpec(memory_space=pltpu.VMEM)],
        out_specs=pl.BlockSpec(memory_space=pltpu.VMEM),
        scratch_shapes=[pltpu.VMEM(gram.shape, jnp.float32), pltpu.VMEM((BLOCK, BLOCK), jnp.float32)],
        compiler_params=pltpu.CompilerParams(vmem_limit_bytes=48 << 20),
    )(gram)


D = 7168
FF = 18432
TILE = 128
decay_rate = 0.95
step_size = 0.3
epsilon = 1e-06

DP = 32
TENSOR = 16
CHIPS = 16
SLAB = RANK // DP
MESH = pl.DeviceIdType.MESH
VMEM = pl.BlockSpec(memory_space=pltpu.VMEM)


def halves(x):
    high = x.astype(jnp.bfloat16)
    return high, (x - high.astype(jnp.float32)).astype(jnp.bfloat16)


def remote(src, dst, send, recv, dp, tensor):
    return pltpu.make_async_remote_copy(
        src_ref=src, dst_ref=dst, send_sem=send, recv_sem=recv, device_id=(dp, tensor), device_id_type=MESH
    )


def slab_rows(dp):
    return pl.ds(pl.multiple_of(SLAB * (CHIPS * lax.rem(dp, 2) + dp // 2), SLAB), SLAB)


def spread_slabs(buffer, dp, tensor, send, recv, pass_send, pass_recv):
    core, chip = lax.rem(dp, 2), dp // 2
    other = dp + 1 - 2 * core

    def rows(which):
        return buffer.at[slab_rows(which), :]

    def copy(step):
        to = lax.rem(chip + step, CHIPS)
        return remote(rows(dp), rows(dp), send.at[step], recv.at[chip], 2 * to + core, tensor)

    def arrival(source):
        return remote(rows(2 * source + core), rows(2 * source + core), send.at[0], recv.at[source], dp, tensor)

    def onward(source):
        return remote(rows(2 * source + core), rows(2 * source + core), pass_send.at[source], pass_recv.at[source], other, tensor)

    def passed(source):
        there = rows(2 * source + 1 - core)
        return remote(there, there, pass_send.at[source], pass_recv.at[source], other, tensor)

    def begin(step, carry):
        copy(step).start()
        return carry

    def forward(step, carry):
        source = lax.rem(chip + CHIPS - step, CHIPS)
        arrival(source).wait_recv()
        onward(source).start()
        return carry

    def finish(step, carry):
        passed(lax.rem(chip + CHIPS - step, CHIPS)).wait_recv()
        return carry

    def drain(step, carry):
        copy(step).wait_send()
        return carry

    def drain_pass(step, carry):
        onward(lax.rem(chip + CHIPS - step, CHIPS)).wait_send()
        return carry

    lax.fori_loop(1, CHIPS, begin, 0)
    onward(chip).start()
    lax.fori_loop(1, CHIPS, forward, 0)
    lax.fori_loop(0, CHIPS, finish, 0)
    lax.fori_loop(1, CHIPS, drain, 0)
    lax.fori_loop(0, CHIPS, drain_pass, 0)


def greet_dp(barrier, dp, tensor):
    core, chip = lax.rem(dp, 2), dp // 2

    def greet(step, carry):
        to = lax.rem(chip + step, CHIPS)
        pl.semaphore_signal(barrier, inc=1, device_id=(2 * to + core, tensor), device_id_type=MESH)
        return carry

    lax.fori_loop(1, CHIPS, greet, 0)
    pl.semaphore_signal(barrier, inc=1, device_id=(dp + 1 - 2 * core, tensor), device_id_type=MESH)


def proj_kernel(momentum, gradient, basis, proj, high, low, basis_high, basis_low, pair_out, pair_in, part, inbox,
                pair_sems, send, recv, all_send, all_recv, pass_send, pass_recv):
    dp, tensor = lax.axis_index("dp"), lax.axis_index("tensor")
    core, chip = lax.rem(dp, 2), dp // 2
    other = dp + 1 - 2 * core
    half = RANK // 2

    barrier = pltpu.get_barrier_semaphore()
    greet_dp(barrier, dp, tensor)

    columns = momentum.shape[1]
    width = columns // 3
    for j in range(3):
        span = pl.ds(j * width, width)
        high[:, span], low[:, span] = halves(momentum[:, span] + gradient[:, span].astype(jnp.float32))
    basis_high[...], basis_low[...] = halves(jnp.transpose(basis[...]))

    def product(first, j):
        span = pl.ds(j * width, width)
        rows = pl.ds(pl.multiple_of(first, half), half)
        return (
            dot_nn(basis_high[rows, :], high[:, span])
            + dot_nn(basis_high[rows, :], low[:, span])
            + dot_nn(basis_low[rows, :], high[:, span])
        )

    for j in range(3):
        pair_out[:, pl.ds(j * width, width)] = product((1 - core) * half, j)
    pl.semaphore_wait(barrier, CHIPS)
    swap = remote(pair_out, pair_in, pair_sems.at[0], pair_sems.at[1], other, tensor)
    swap.start()
    mine = [product(core * half, j) for j in range(3)]
    swap.wait_recv()
    for j in range(3):
        span = pl.ds(j * width, width)
        part[:, span] = (mine[j] + pair_in[:, span]).astype(jnp.bfloat16)

    def slab(which):
        return part.at[pl.ds(pl.multiple_of(which * SLAB, SLAB), SLAB), :]

    def copy(step):
        to = lax.rem(chip + step, CHIPS)
        return remote(slab(to), inbox.at[chip], send.at[step], recv.at[chip], 2 * to + core, tensor)

    def begin(step, carry):
        copy(step).start()
        return carry

    def arrive(step, total):
        source = lax.rem(chip + CHIPS - step, CHIPS)
        remote(inbox.at[source], inbox.at[source], send.at[0], recv.at[source], other, tensor).wait_recv()
        return total + inbox[source].astype(jnp.float32)

    def drain(step, carry):
        copy(step).wait_send()
        return carry

    lax.fori_loop(1, CHIPS, begin, 0)
    total = part[pl.ds(pl.multiple_of(chip * SLAB, SLAB), SLAB), :].astype(jnp.float32)
    total = lax.fori_loop(1, CHIPS, arrive, total)
    proj[slab_rows(dp), :] = total.astype(jnp.bfloat16)
    spread_slabs(proj, dp, tensor, all_send, all_recv, pass_send, pass_recv)
    lax.fori_loop(1, CHIPS, drain, 0)
    swap.wait_send()


def proj_transposed(momentum, gradient, basis):
    rows, columns = momentum.shape
    half = RANK // 2
    dma = pltpu.SemaphoreType.DMA
    return pl.pallas_call(
        proj_kernel,
        out_shape=jax.ShapeDtypeStruct((RANK, columns), jnp.bfloat16),
        in_specs=[VMEM] * 3,
        out_specs=VMEM,
        scratch_shapes=[
            pltpu.VMEM((rows, columns), jnp.bfloat16),
            pltpu.VMEM((rows, columns), jnp.bfloat16),
            pltpu.VMEM((RANK, rows), jnp.bfloat16),
            pltpu.VMEM((RANK, rows), jnp.bfloat16),
            pltpu.VMEM((half, columns), jnp.float32),
            pltpu.VMEM((half, columns), jnp.float32),
            pltpu.VMEM((half, columns), jnp.bfloat16),
            pltpu.VMEM((CHIPS, SLAB, columns), jnp.bfloat16),
            dma((2,)), dma((CHIPS,)), dma((CHIPS,)), dma((CHIPS,)), dma((CHIPS,)), dma((CHIPS,)), dma((CHIPS,)),
        ],
        compiler_params=pltpu.CompilerParams(collective_id=0, has_side_effects=True, vmem_limit_bytes=48 << 20),
    )(momentum, gradient, basis)


OWNERS = 8
WIDE_ROWS, WIDE_COLUMNS = 64, 128


def sums_kernel(momentum, gradient, proj, gram, wide, gram_part, gram_inbox, wide_part, wide_inbox, wide_all,
                tile_send, tile_recv, back_send, back_recv, wide_send, wide_recv, out_send, out_recv,
                all_send, all_recv, pass_send, pass_recv):
    dp, tensor = lax.axis_index("dp"), lax.axis_index("tensor")
    rows = momentum.shape[0]
    barrier = pltpu.get_barrier_semaphore()
    greet_dp(barrier, dp, tensor)

    def greet(step, carry):
        to = lax.rem(tensor + step, TENSOR)
        pl.semaphore_signal(barrier, inc=1, device_id=(dp, to), device_id_type=MESH)
        return carry

    lax.fori_loop(1, TENSOR, greet, 0)

    gram_part[...] = dot_nt(proj[slab_rows(dp), :], proj[...])
    pl.semaphore_wait(barrier, CHIPS + TENSOR - 1)

    def tile(ref, first, owner):
        return ref.at[
            pl.ds(pl.multiple_of(first + 8 * (owner // 4), 8), 8), pl.ds(pl.multiple_of(128 * lax.rem(owner, 4), 128), 128)
        ]

    def tile_copy(owner):
        return remote(tile(gram_part, 0, owner), gram_inbox.at[tensor], tile_send.at[owner], tile_recv.at[tensor], dp, owner)

    def tile_begin(owner, carry):
        @pl.when(owner != tensor)
        def _():
            tile_copy(owner).start()

        return carry

    lax.fori_loop(0, OWNERS, tile_begin, 0)

    high, low = halves(momentum[...] + gradient[...].astype(jnp.float32))
    wide_part[:rows, :] = (dot_nt(high, proj[...]) + dot_nt(low, proj[...])).astype(jnp.bfloat16)
    wide_part[rows:, :] = jnp.zeros((wide_part.shape[0] - rows, RANK), jnp.bfloat16)

    def piece(ref, which):
        return ref.at[
            pl.ds(pl.multiple_of(WIDE_ROWS * (which // 4), WIDE_ROWS), WIDE_ROWS),
            pl.ds(pl.multiple_of(WIDE_COLUMNS * lax.rem(which, 4), WIDE_COLUMNS), WIDE_COLUMNS),
        ]

    def wide_copy(step):
        to = lax.rem(tensor + step, TENSOR)
        return remote(piece(wide_part, to), wide_inbox.at[tensor], wide_send.at[step], wide_recv.at[tensor], dp, to)

    def wide_begin(step, carry):
        wide_copy(step).start()
        return carry

    lax.fori_loop(1, TENSOR, wide_begin, 0)

    first = SLAB * (CHIPS * lax.rem(dp, 2) + dp // 2)

    def back_copy(step):
        to = lax.rem(tensor + step, TENSOR)
        here = tile(gram, first, tensor)
        return remote(here, here, back_send.at[step], back_recv.at[tensor], dp, to)

    @pl.when(tensor < OWNERS)
    def _():
        def arrive(step, total):
            source = lax.rem(tensor + step, TENSOR)
            there = gram_inbox.at[source]
            remote(there, there, tile_send.at[0], tile_recv.at[source], dp, tensor).wait_recv()
            return total + gram_inbox[source]

        def back_begin(step, carry):
            back_copy(step).start()
            return carry

        total = lax.fori_loop(1, TENSOR, arrive, tile(gram_part, 0, tensor)[...])
        tile(gram, first, tensor)[...] = total
        lax.fori_loop(1, TENSOR, back_begin, 0)

    def wide_arrive(step, total):
        source = lax.rem(tensor + step, TENSOR)
        there = wide_inbox.at[source]
        remote(there, there, wide_send.at[0], wide_recv.at[source], dp, tensor).wait_recv()
        return total + wide_inbox[source].astype(jnp.float32)

    def out_copy(step):
        to = lax.rem(tensor + step, TENSOR)
        here = piece(wide_all, tensor)
        return remote(here, here, out_send.at[step], out_recv.at[tensor], dp, to)

    def out_begin(step, carry):
        out_copy(step).start()
        return carry

    def back_arrive(owner, carry):
        @pl.when(owner != tensor)
        def _():
            there = tile(gram, first, owner)
            remote(there, there, back_send.at[0], back_recv.at[owner], dp, tensor).wait_recv()

        return carry

    lax.fori_loop(0, OWNERS, back_arrive, 0)
    spread_slabs(gram, dp, tensor, all_send, all_recv, pass_send, pass_recv)

    piece(wide_all, tensor)[...] = lax.fori_loop(
        1, TENSOR, wide_arrive, piece(wide_part, tensor)[...].astype(jnp.float32)
    )
    lax.fori_loop(1, TENSOR, out_begin, 0)

    def out_arrive(step, carry):
        source = lax.rem(tensor + step, TENSOR)
        there = piece(wide_all, source)
        remote(there, there, out_send.at[0], out_recv.at[source], dp, tensor).wait_recv()
        return carry

    lax.fori_loop(1, TENSOR, out_arrive, 0)
    wide[...] = wide_all[:rows, :]

    def tile_drain(owner, carry):
        @pl.when(owner != tensor)
        def _():
            tile_copy(owner).wait_send()

        return carry

    def drain(step, carry):
        wide_copy(step).wait_send()
        out_copy(step).wait_send()

        @pl.when(tensor < OWNERS)
        def _():
            back_copy(step).wait_send()

        return carry

    lax.fori_loop(0, OWNERS, tile_drain, 0)
    lax.fori_loop(1, TENSOR, drain, 0)


def gram_and_wide(momentum, gradient, proj):
    rows = momentum.shape[0]
    padded = TENSOR // 4 * WIDE_ROWS
    dma = pltpu.SemaphoreType.DMA
    return pl.pallas_call(
        sums_kernel,
        out_shape=(jax.ShapeDtypeStruct((RANK, RANK), jnp.float32), jax.ShapeDtypeStruct((rows, RANK), jnp.float32)),
        in_specs=[VMEM] * 3,
        out_specs=(VMEM, VMEM),
        scratch_shapes=[
            pltpu.VMEM((SLAB, RANK), jnp.float32),
            pltpu.VMEM((TENSOR, 8, 128), jnp.float32),
            pltpu.VMEM((padded, RANK), jnp.bfloat16),
            pltpu.VMEM((TENSOR, WIDE_ROWS, WIDE_COLUMNS), jnp.bfloat16),
            pltpu.VMEM((padded, RANK), jnp.float32),
            dma((OWNERS,)), dma((TENSOR,)), dma((TENSOR,)), dma((OWNERS,)),
            dma((TENSOR,)), dma((TENSOR,)), dma((TENSOR,)), dma((TENSOR,)),
            dma((CHIPS,)), dma((CHIPS,)), dma((CHIPS,)), dma((CHIPS,)),
        ],
        compiler_params=pltpu.CompilerParams(collective_id=1, has_side_effects=True, vmem_limit_bytes=48 << 20),
    )(momentum, gradient, proj)


def basis_kernel(wide, inverse, back, new_basis, inbox, send, recv):
    dp, tensor = lax.axis_index("dp"), lax.axis_index("tensor")
    barrier = pltpu.get_barrier_semaphore()

    def greet(step, carry):
        pl.semaphore_signal(barrier, inc=1, device_id=(lax.rem(dp + step, DP), tensor), device_id_type=MESH)
        return carry

    lax.fori_loop(1, DP, greet, 0)
    own = dot_nt(wide[...], inverse[...], HIGHEST)
    back[...] = own
    inbox[dp] = jnp.sum((own * own).reshape(own.shape[0] // 8, 8, own.shape[1]), axis=0)
    pl.semaphore_wait(barrier, DP - 1)

    def copy(step):
        return remote(inbox.at[dp], inbox.at[dp], send.at[step], recv.at[dp], lax.rem(dp + step, DP), tensor)

    def begin(step, carry):
        copy(step).start()
        return carry

    def arrive(step, carry):
        there = inbox.at[lax.rem(dp + step, DP)]
        remote(there, there, send.at[0], recv.at[lax.rem(dp + step, DP)], dp, tensor).wait_recv()
        return carry

    def drain(step, carry):
        copy(step).wait_send()
        return carry

    lax.fori_loop(1, DP, begin, 0)
    lax.fori_loop(1, DP, arrive, 0)
    total = inbox[0]
    for source in range(1, DP):
        total += inbox[source]
    colsq = jnp.sum(total, axis=0, keepdims=True)
    new_basis[...] = own / jnp.sqrt(colsq + epsilon)
    lax.fori_loop(1, DP, drain, 0)


def back_and_basis(wide, inverse):
    dma = pltpu.SemaphoreType.DMA
    return pl.pallas_call(
        basis_kernel,
        out_shape=(jax.ShapeDtypeStruct(wide.shape, jnp.float32),) * 2,
        in_specs=[VMEM] * 2,
        out_specs=(VMEM, VMEM),
        scratch_shapes=[pltpu.VMEM((DP, 8, RANK), jnp.float32), dma((DP,)), dma((DP,))],
        compiler_params=pltpu.CompilerParams(collective_id=2, has_side_effects=True, vmem_limit_bytes=48 << 20),
    )(wide, inverse)


def quantize(block):
    rows = block.shape[0]
    width = block.shape[1]
    tiles = block.astype(jnp.float32).reshape(rows, width // TILE, TILE)
    largest = jnp.max(jnp.abs(tiles), axis=2)
    values = (tiles / (largest[:, :, None] + epsilon)).astype(jnp.bfloat16)
    return (values.reshape(rows, width), largest)


def on_device(weight, gradient, momentum, basis):
    high = lax.Precision.HIGH
    proj = proj_transposed(momentum, gradient, basis)
    gram, wide = gram_and_wide(momentum, gradient, proj)
    inverse = inverse_factor(gram)
    back, new_basis = back_and_basis(wide, inverse)
    inverse_high, inverse_low = halves(inverse)
    ortho = dot_nn(inverse_high, proj) + dot_nn(inverse_low, proj)
    buffer = momentum + gradient.astype(jnp.float32)
    new_momentum = buffer - (1.0 - decay_rate) * jnp.dot(back, ortho, precision=high)
    factor = step_size * math.sqrt(FF / D)
    updated = (weight.astype(jnp.float32) - factor * jnp.dot(new_basis, ortho, precision=high)).astype(jnp.bfloat16)
    full_rows = lax.all_to_all(updated.T, "dp", split_axis=0, concat_axis=1, tiled=True)
    row_values, row_scales = quantize(full_rows)
    full_columns = lax.all_to_all(updated, "tensor", split_axis=0, concat_axis=1, tiled=True)
    column_values, column_scales = quantize(full_columns)
    return (new_momentum, new_basis, row_values, row_scales, column_values, column_scales)


def solution(mesh):
    placed = (P("dp", "tensor"), P("dp", "tensor"), P("dp", "tensor"), P("dp", None))
    return jax.shard_map(
        on_device,
        mesh=mesh,
        in_specs=placed,
        out_specs=(
            P("dp", "tensor"),
            P("dp", None),
            P(("tensor", "dp"), None),
            P(("tensor", "dp"), None),
            P(("dp", "tensor"), None),
            P(("dp", "tensor"), None),
        ),
        check_vma=False,
    )
```

time: 889 us -> 225 us (0.25)
  waiting for transfers between devices: 576 us -> 22.6 us
  Pallas kernels: 0 us -> 154 us
  other arithmetic: 131 us -> 4.44 us
  blocking collectives: 76.1 us -> 0 us
  matrix products: 45.4 us -> 6.73 us
  between operations: 17.1 us -> 0.9 us
    psum x3 -> x0, waiting for transfers between devices: 553 us -> none  [the longest x1 285 us: on_device(): proj = lax.psum(jnp.dot(buffer.T, basis, precision=highest), 'dp')]
    pallas_call x0 -> x4, Pallas kernels: none -> 154 us  [the longest x1 50.5 us: gram_and_wide(): pl.pallas_call(sums_kernel, out_shape=(jax.ShapeDtypeStruct((RANK, RANK),...]
    another operation x17 -> x0, other arithmetic: 123 us -> none  [the longest x14 80.5 us: orthonormal(): lower = jnp.linalg.cholesky(gram)]
    psum x1 -> x0, blocking collectives: 76.1 us -> none  [on_device(): colsq = lax.psum(jnp.sum(back * back, axis=0), 'dp')]
    another operation x13 -> x0, matrix products: 21.1 us -> none  [the longest x7 13.1 us: orthonormal(): return jax.scipy.linalg.solve_triangular(lower, proj.T, lower=True).T]
    dot_general x5 -> x4, matrix products: 24.3 us -> 6.73 us  [the longest x1 3.82 us: on_device(): jnp.dot(back, ortho, precision=high)]
    another operation x17 -> x0, local copies, waits for them, and re-layouts: 12.6 us -> none
  transfers between devices with their start and end apart: 5 -> 2, of which waited for: 5 -> 2; matrix products, arithmetic and copies ran while one was open for 2% -> 5% of each run, Pallas kernels for 0% -> 0%
where the time goes in v1:
time: 225 us; the launch traced here: 224 us
  Pallas kernels  154 us (68%)
  waiting for transfers between devices  22.6 us (10%)
  local copies, waits for them, and re-layouts  19.1 us (8%)
  starting transfers between devices  16.2 us (7%)
  matrix products  6.73 us (3%)
  other arithmetic  4.44 us (2%)
    pallas_call x1, Pallas kernels, gram_and_wide(): pl.pallas_call(sums_kernel, out_shape=(jax.ShapeDtypeStruct((RANK, RANK),...  50.5 us
    pallas_call x1, Pallas kernels, proj_transposed(): pl.pallas_call(proj_kernel, out_shape=jax.ShapeDtypeStruct((RANK, columns...  50.3 us
    pallas_call x1, Pallas kernels, inverse_factor(): pl.pallas_call(cholesky_kernel, out_shape=jax.ShapeDtypeStruct(gram.shape...  30.5 us
    pallas_call x1, Pallas kernels, back_and_basis(): pl.pallas_call(basis_kernel, out_shape=(jax.ShapeDtypeStruct(wide.shape,...  22.4 us
    all_to_all x1, waiting for transfers between devices, on_device(): lax.all_to_all(updated.T, 'dp', split_axis=0, concat_axis=1, tiled=True)  14.7 us
    all_to_all x1, starting transfers between devices, on_device(): lax.all_to_all(updated.T, 'dp', split_axis=0, concat_axis=1, tiled=True)  10.3 us
    unnamed x29, local copies, waits for them, and re-layouts  8.9 us
    all_to_all x1, waiting for transfers between devices, on_device(): lax.all_to_all(updated, 'tensor', split_axis=0, concat_axis=1, tiled=True)  7.89 us
  transfers between devices with their start and end apart: 2, of which 2 were waited for; matrix products, arithmetic and copies ran while one was open for 5% of the time, Pallas kernels for 0%

profile of v1, /device:TPU:1, one launch (start us, length us, event | category | flops | bytes accessed | tf_op | source)
XLA Modules:
  0.0 223.7 jit_solution(7607020501359874453)
XLA Ops:
  0.6 1.2 copy-done
  1.9 1.0 copy-done.2
  2.9 1.0 copy-done.4
  3.9 50.3 %shard_map.91.proj = bf16[512,1152]{1,0:T(8,128)(2,1)S(1)} custom-call(f32[224,1152]{1,0:T(8,128)S(1)} %copy-done, bf16[224,1152]{1,0:T(8,128)(2,1)S(1)} %copy-done.2, f32[224,512]{1,0:T(8,128)S(1)} %copy-done.4), custom_call_target="tpu_custom_call" | custom-call | tf_op jit(solution)/shard_map/pallas_call | solution.py:264
  54.2 50.5 %shard_map.92 = (f32[512,512]{1,0:T(8,128)S(1)}, f32[224,512]{1,0:T(8,128)S(1)}) custom-call(f32[224,1152]{1,0:T(8,128)S(1)} %copy-done, bf16[224,1152]{1,0:T(8,128)(2,1)S(1)} %copy-done.2, bf16[512,1152]{1,0:T(8,128)(2,1)S(1)} %shard_map.91.proj), custom_call_target="tpu_custom_call" | custom-call | tf_op jit(solution)/shard_map/pallas_call | solution.py:431
  104.7 30.5 %shard_map.93.inverse = f32[512,512]{1,0:T(8,128)S(1)} custom-call(f32[512,512]{1,0:T(8,128)S(1)} %get-tuple-element.11.gram_ref), custom_call_target="tpu_custom_call" | custom-call | tf_op jit(solution)/shard_map/pallas_call | solution.py:91
  135.3 0.8 fusion.6
  136.1 22.4 %shard_map.94 = (f32[224,512]{1,0:T(8,128)S(1)}, f32[224,512]{1,0:T(8,128)S(1)}) custom-call(f32[224,512]{1,0:T(8,128)S(1)} %get-tuple-element.10.wide, f32[512,512]{1,0:T(8,128)S(1)} %shard_map.93.inverse), custom_call_target="tpu_custom_call" | custom-call | tf_op jit(solution)/shard_map/pallas_call | solution.py:492
  158.5 0.8 convolution_add_fusion
  159.4 1.4 copy-done.5
  160.8 1.2 fusion.2
  162.0 1.0 all_to_all.22
  163.0 5.9 %all-to-all-start.1 = ((bf16[16,14,1152]{2,1,0:T(8,128)(2,1)}), bf16[16,14,1152]{2,1,0:T(8,128)(2,1)S(1)}, u32[]{:S(2)}, u32[]{:S(2)}) async-start(bf16[16,14,1152]{2,1,0:T(8,128)(2,1)} %all_to_all.22), calls=%async_computation.1 | async-start | bytes 1179648 | tf_op jit(solution)/shard_map/all_to_all | solution.py:525
  168.9 2.2 copy.15
  171.1 2.1 all_to_all.20
  173.3 3.8 %fusion.1 = f32[224,1152]{1,0:T(8,128)} fusion(f32[224,512]{1,0:T(8,128)S(1)} %get-tuple-element.12, f32[512,1152]{1,0:T(8,128)} %copy-done.5, f32[224,1152]{1,0:T(8,128)S(1)} %copy-done.1, bf16[224,1152]{1,0:T(8,128)(2,1)S(1)} %copy-done.3), kind=kOutput, calls=%fused_computation.4 | convolution fusion | flops 793755648 | bytes 5398528 | tf_op jit(solution)/shard_map/dot_general | solution.py:520
  177.1 7.9 %all-to-all-done.1 = bf16[16,14,1152]{2,1,0:T(8,128)(2,1)S(1)} async-done(((bf16[16,14,1152]{2,1,0:T(8,128)(2,1)}), bf16[16,14,1152]{2,1,0:T(8,128)(2,1)S(1)}, u32[]{:S(2)}, u32[]{:S(2)}) %all-to-all-start.1) | async-done | bytes 516128 | tf_op jit(solution)/shard_map/all_to_all | solution.py:525
  185.0 10.3 %all-to-all-start = ((bf16[32,36,224]{2,1,0:T(8,128)(2,1)}), bf16[32,36,224]{2,1,0:T(8,128)(2,1)S(1)}, u32[]{:S(2)}, u32[]{:S(2)}) async-start(bf16[32,36,224]{2,1,0:T(8,128)(2,1)} %all_to_all.20), calls=%async_computation | async-start | bytes 1310720 | tf_op jit(solution)/shard_map/all_to_all | solution.py:523
  195.8 1.4 copy.21
  197.3 0.3 copy.19
  197.7 0.5 reduce_max.19
  198.8 0.4 copy.22
  199.2 0.9 copy-done.6
  200.1 1.0 divide_convert_fusion
  201.1 14.7 %all-to-all-done = bf16[32,36,224]{2,1,0:T(8,128)(2,1)S(1)} async-done(((bf16[32,36,224]{2,1,0:T(8,128)(2,1)}), bf16[32,36,224]{2,1,0:T(8,128)(2,1)S(1)}, u32[]{:S(2)}, u32[]{:S(2)}) %all-to-all-start) | async-done | bytes 516128 | tf_op jit(solution)/shard_map/all_to_all | solution.py:523
  215.9 0.4 copy.16
  216.3 0.8 reshape.44
  217.2 0.4 copy.17
  217.6 2.0 abs.20
  219.5 1.6 reduce_max.18
  221.9 1.0 divide_convert_fusion.1
  222.9 0.8 copy.24
  (31 shorter events, 2.3 us)
Async XLA Ops:
  0.6 1.2 copy-start
  1.9 1.0 copy-start.2
  2.9 1.0 copy-start.4
  158.5 2.3 %copy-start.8 = (bf16[224,1152]{1,0:T(8,128)(2,1)S(1)}, bf16[224,1152]{1,0:T(8,128)(2,1)}, u32[]{:S(2)}) copy-start(bf16[224,1152]{1,0:T(8,128)(2,1)} %param.4) | copy-start | bytes 1548292
  159.4 1.4 copy-start.5
  162.0 1.0 copy-start.7
  163.0 22.0 %all-to-all-start.1 = ((bf16[16,14,1152]{2,1,0:T(8,128)(2,1)}), bf16[16,14,1152]{2,1,0:T(8,128)(2,1)S(1)}, u32[]{:S(2)}, u32[]{:S(2)}) async-start(bf16[16,14,1152]{2,1,0:T(8,128)(2,1)} %all_to_all.22), calls=%async_computation.1 | async-start | bytes 1179648 | tf_op jit(solution)/shard_map/all_to_all | solution.py:525
  168.9 4.4 %copy-start.1 = (f32[224,1152]{1,0:T(8,128)S(1)}, f32[224,1152]{1,0:T(8,128)}, u32[]{:S(2)}) copy-start(f32[224,1152]{1,0:T(8,128)} %momentum.3) | copy-start | bytes 3096580
  168.9 4.4 %copy-start.3 = (bf16[224,1152]{1,0:T(8,128)(2,1)S(1)}, bf16[224,1152]{1,0:T(8,128)(2,1)}, u32[]{:S(2)}) copy-start(bf16[224,1152]{1,0:T(8,128)(2,1)} %gradient.3) | copy-start | bytes 1548292
  185.0 30.8 %all-to-all-start = ((bf16[32,36,224]{2,1,0:T(8,128)(2,1)}), bf16[32,36,224]{2,1,0:T(8,128)(2,1)S(1)}, u32[]{:S(2)}, u32[]{:S(2)}) async-start(bf16[32,36,224]{2,1,0:T(8,128)(2,1)} %all_to_all.20), calls=%async_computation | async-start | bytes 1310720 | tf_op jit(solution)/shard_map/all_to_all | solution.py:523
  198.2 0.6 copy-start.10
  198.8 1.3 copy-start.6
  221.1 0.6 copy-start.9

commit v2 on v1

--- a/solution.py
+++ b/solution.py
@@ -447,84 +447,218 @@
     )(momentum, gradient, proj)
 
 
-def basis_kernel(wide, inverse, back, new_basis, inbox, send, recv):
+CHUNK = 48
+ROWS_OUT = FF // TENSOR // DP
+COLUMNS_OUT = D // DP // TENSOR
+TURN = 32
+
+
+def apply_kernel(weight, momentum, gradient, wide, inverse, proj,
+                 new_momentum, new_basis, row_values, row_scales, column_values, column_scales,
+                 back_high, basis_high, basis_low, ortho_high, ortho_low, square_inbox, update, turned, flipped, row_out, row_in, column_out, column_in,
+                 square_send, square_recv, row_send, row_recv, column_send, column_recv):
     dp, tensor = lax.axis_index("dp"), lax.axis_index("tensor")
+    rows, columns = weight.shape
+    width = columns // 3
     barrier = pltpu.get_barrier_semaphore()
 
-    def greet(step, carry):
+    def greet_rows(step, carry):
         pl.semaphore_signal(barrier, inc=1, device_id=(lax.rem(dp + step, DP), tensor), device_id_type=MESH)
         return carry
 
-    lax.fori_loop(1, DP, greet, 0)
-    own = dot_nt(wide[...], inverse[...], HIGHEST)
-    back[...] = own
-    inbox[dp] = jnp.sum((own * own).reshape(own.shape[0] // 8, 8, own.shape[1]), axis=0)
-    pl.semaphore_wait(barrier, DP - 1)
-
-    def copy(step):
-        return remote(inbox.at[dp], inbox.at[dp], send.at[step], recv.at[dp], lax.rem(dp + step, DP), tensor)
-
-    def begin(step, carry):
-        copy(step).start()
-        return carry
-
-    def arrive(step, carry):
-        there = inbox.at[lax.rem(dp + step, DP)]
-        remote(there, there, send.at[0], recv.at[lax.rem(dp + step, DP)], dp, tensor).wait_recv()
-        return carry
-
-    def drain(step, carry):
-        copy(step).wait_send()
-        return carry
-
-    lax.fori_loop(1, DP, begin, 0)
-    lax.fori_loop(1, DP, arrive, 0)
-    total = inbox[0]
+    def greet_columns(step, carry):
+        pl.semaphore_signal(barrier, inc=1, device_id=(dp, lax.rem(tensor + step, TENSOR)), device_id_type=MESH)
+        return carry
+
+    lax.fori_loop(1, DP, greet_rows, 0)
+    lax.fori_loop(1, TENSOR, greet_columns, 0)
+
+    inverse_high, inverse_low = halves(inverse[...])
+    wide_high, wide_low = halves(wide[...])
+    back = dot_nt(wide_high, inverse_high) + dot_nt(wide_low, inverse_high) + dot_nt(wide_high, inverse_low)
+    squares = jnp.sum(jnp.sum((back * back).reshape(rows // 8, 8, RANK), axis=0), axis=0, keepdims=True)
+    lanes = RANK // 4
+    square_inbox[dp] = jnp.concatenate(
+        [squares[:, j * lanes:(j + 1) * lanes] for j in range(4)] + [jnp.zeros((4, lanes), jnp.float32)], axis=0
+    )
+    pl.semaphore_wait(barrier, DP + TENSOR - 2)
+
+    def square_copy(step):
+        here = square_inbox.at[dp]
+        return remote(here, here, square_send.at[step], square_recv.at[dp], lax.rem(dp + step, DP), tensor)
+
+    def square_begin(step, carry):
+        square_copy(step).start()
+        return carry
+
+    lax.fori_loop(1, DP, square_begin, 0)
+    back_high[...] = back.astype(jnp.bfloat16)
+    for j in range(3):
+        span = pl.ds(j * width, width)
+        ortho = dot_nn(inverse_high, proj[:, span]) + dot_nn(inverse_low, proj[:, span])
+        ortho_high[:, span], ortho_low[:, span] = halves(ortho)
+
+    def square_arrive(step, carry):
+        source = lax.rem(dp + step, DP)
+        there = square_inbox.at[source]
+        remote(there, there, square_send.at[0], square_recv.at[source], dp, tensor).wait_recv()
+        return carry
+
+    lax.fori_loop(1, DP, square_arrive, 0)
+    total = square_inbox[0]
     for source in range(1, DP):
-        total += inbox[source]
-    colsq = jnp.sum(total, axis=0, keepdims=True)
-    new_basis[...] = own / jnp.sqrt(colsq + epsilon)
-    lax.fori_loop(1, DP, drain, 0)
-
-
-def back_and_basis(wide, inverse):
+        total += square_inbox[source]
+    colsq = jnp.concatenate([total[j:j + 1, :] for j in range(4)], axis=1)
+    fresh = back / jnp.sqrt(colsq + epsilon)
+    new_basis[...] = fresh
+    basis_high[...], basis_low[...] = halves(fresh)
+
+    factor = step_size * math.sqrt(FF / D)
+    shift = lax.rem(3 * dp, 4)
+    for j in range(3):
+        span = pl.ds(j * width, width)
+        product = (
+            dot_nn(basis_high[...], ortho_high[:, span])
+            + dot_nn(basis_low[...], ortho_high[:, span])
+            + dot_nn(basis_high[...], ortho_low[:, span])
+        )
+        update[:, span] = weight[:, span].astype(jnp.float32) - factor * product
+
+    def row_copy(step):
+        to = lax.rem(dp + step, DP)
+        return remote(row_out.at[to], row_in.at[dp], row_send.at[step], row_recv.at[dp], to, tensor)
+
+    def column_copy(step):
+        to = lax.rem(tensor + step, TENSOR)
+        return remote(column_out.at[to], column_in.at[tensor], column_send.at[step], column_recv.at[tensor], dp, to)
+
+    def row_begin(step, carry):
+        row_copy(step).start()
+        return carry
+
+    def column_begin(step, carry):
+        column_copy(step).start()
+        return carry
+
+    column_out[...] = jnp.zeros(column_out.shape, jnp.bfloat16)
+    row_out[...] = jnp.zeros(row_out.shape, jnp.bfloat16)
+    pieces = rows // TURN
+    for i in range(pieces + 1):
+        to = pl.ds(pl.multiple_of(TURN * lax.rem(i + shift, pieces + 1), TURN), TURN)
+        turned[to, :] = update[pl.ds(TURN * i, TURN), :] if i < pieces else jnp.zeros((TURN, columns), jnp.float32)
+    for to in range(TENSOR):
+        column_out[to, pl.ds(0, COLUMNS_OUT), :] = update[pl.ds(COLUMNS_OUT * to, COLUMNS_OUT), :].astype(jnp.bfloat16)
+    lax.fori_loop(1, TENSOR, column_begin, 0)
+    for j in range(columns // TILE):
+        flipped[pl.ds(TILE * j, TILE), :] = jnp.transpose(turned[:, pl.ds(TILE * j, TILE)])
+    for to in range(DP):
+        row_out[to, pl.ds(0, ROWS_OUT), :] = flipped[pl.ds(ROWS_OUT * to, ROWS_OUT), :].astype(jnp.bfloat16)
+    lax.fori_loop(1, DP, row_begin, 0)
+    column_in[tensor] = column_out[tensor]
+    row_in[dp] = row_out[dp]
+
+    for j in range(3):
+        span = pl.ds(j * width, width)
+        product = dot_nn(back_high[...], ortho_high[:, span])
+        new_momentum[:, span] = momentum[:, span] + gradient[:, span].astype(jnp.float32) - (1.0 - decay_rate) * product
+
+    def column_arrive(step, carry):
+        source = lax.rem(tensor + step, TENSOR)
+        there = column_in.at[source]
+        remote(there, there, column_send.at[0], column_recv.at[source], dp, tensor).wait_recv()
+        return carry
+
+    def row_arrive(step, carry):
+        source = lax.rem(dp + step, DP)
+        there = row_in.at[source]
+        remote(there, there, row_send.at[0], row_recv.at[source], dp, tensor).wait_recv()
+        return carry
+
+    def scaled(tile):
+        largest = jnp.max(jnp.abs(tile), axis=1, keepdims=True)
+        return (tile * (1.0 / (largest + epsilon))).astype(jnp.bfloat16), largest
+
+    lax.fori_loop(1, TENSOR, column_arrive, 0)
+    count = columns // TILE
+    lane_of = lax.broadcasted_iota(jnp.int32, (16, 256), 1)
+    scales = jnp.zeros((16, 256), jnp.float32)
+    for source in range(TENSOR):
+        for j in range(count):
+            values, largest = scaled(column_in[source, :, pl.ds(TILE * j, TILE)].astype(jnp.float32))
+            column_values[:, pl.ds(columns * source + TILE * j, TILE)] = values[:COLUMNS_OUT]
+            scales = jnp.where(lane_of == count * source + j, largest, scales)
+    column_scales[...] = scales[:COLUMNS_OUT, :FF // TILE]
+
+    lax.fori_loop(1, DP, row_arrive, 0)
+    lane_of = lax.broadcasted_iota(jnp.int32, (CHUNK, TILE), 1)
+    scales = jnp.zeros((CHUNK, TILE), jnp.float32)
+    for tile in range(D // TILE):
+        source = TILE * tile // rows
+        part = lambda which: row_in[which, :, pl.ds(TILE * ((tile - rows * which // TILE) % 2), TILE)].astype(jnp.float32)
+        block = part(source)
+        bound = rows * (source + 1) - TILE * tile
+        if bound < TILE:
+            block = jnp.where(lane_of < bound, block, part(source + 1))
+        values, largest = scaled(block)
+        row_values[:, pl.ds(TILE * tile, TILE)] = values[:ROWS_OUT]
+        scales = jnp.where(lane_of == tile, largest, scales)
+    row_scales[...] = scales[:ROWS_OUT, :D // TILE]
+
+    def square_drain(step, carry):
+        square_copy(step).wait_send()
+        row_copy(step).wait_send()
+        return carry
+
+    def column_drain(step, carry):
+        column_copy(step).wait_send()
+        return carry
+
+    lax.fori_loop(1, DP, square_drain, 0)
+    lax.fori_loop(1, TENSOR, column_drain, 0)
+
+
+def apply_update(weight, momentum, gradient, wide, inverse, proj):
+    rows, columns = weight.shape
     dma = pltpu.SemaphoreType.DMA
+    f32, bf16 = jnp.float32, jnp.bfloat16
+    shape = jax.ShapeDtypeStruct
     return pl.pallas_call(
-        basis_kernel,
-        out_shape=(jax.ShapeDtypeStruct(wide.shape, jnp.float32),) * 2,
-        in_specs=[VMEM] * 2,
-        out_specs=(VMEM, VMEM),
-        scratch_shapes=[pltpu.VMEM((DP, 8, RANK), jnp.float32), dma((DP,)), dma((DP,))],
+        apply_kernel,
+        out_shape=(
+            shape((rows, columns), f32),
+            shape((rows, RANK), f32),
+            shape((ROWS_OUT, D), bf16),
+            shape((ROWS_OUT, D // TILE), f32),
+            shape((COLUMNS_OUT, FF), bf16),
+            shape((COLUMNS_OUT, FF // TILE), f32),
+        ),
+        in_specs=[VMEM] * 6,
+        out_specs=(VMEM,) * 6,
+        scratch_shapes=[
+            pltpu.VMEM((rows, RANK), bf16),
+            pltpu.VMEM((rows, RANK), bf16),
+            pltpu.VMEM((rows, RANK), bf16),
+            pltpu.VMEM((RANK, columns), bf16),
+            pltpu.VMEM((RANK, columns), bf16),
+            pltpu.VMEM((DP, 8, RANK // 4), f32),
+            pltpu.VMEM((rows, columns), f32),
+            pltpu.VMEM((rows + TURN, columns), f32),
+            pltpu.VMEM((columns, rows + TURN), f32),
+            pltpu.VMEM((DP, CHUNK, rows + TURN), bf16),
+            pltpu.VMEM((DP, CHUNK, rows + TURN), bf16),
+            pltpu.VMEM((TENSOR, 16, columns), bf16),
+            pltpu.VMEM((TENSOR, 16, columns), bf16),
+            dma((DP,)), dma((DP,)), dma((DP,)), dma((DP,)), dma((TENSOR,)), dma((TENSOR,)),
+        ],
         compiler_params=pltpu.CompilerParams(collective_id=2, has_side_effects=True, vmem_limit_bytes=48 << 20),
-    )(wide, inverse)
-
-
-def quantize(block):
-    rows = block.shape[0]
-    width = block.shape[1]
-    tiles = block.astype(jnp.float32).reshape(rows, width // TILE, TILE)
-    largest = jnp.max(jnp.abs(tiles), axis=2)
-    values = (tiles / (largest[:, :, None] + epsilon)).astype(jnp.bfloat16)
-    return (values.reshape(rows, width), largest)
+    )(weight, momentum, gradient, wide, inverse, proj)
 
 
 def on_device(weight, gradient, momentum, basis):
-    high = lax.Precision.HIGH
     proj = proj_transposed(momentum, gradient, basis)
     gram, wide = gram_and_wide(momentum, gradient, proj)
     inverse = inverse_factor(gram)
-    back, new_basis = back_and_basis(wide, inverse)
-    inverse_high, inverse_low = halves(inverse)
-    ortho = dot_nn(inverse_high, proj) + dot_nn(inverse_low, proj)
-    buffer = momentum + gradient.astype(jnp.float32)
-    new_momentum = buffer - (1.0 - decay_rate) * jnp.dot(back, ortho, precision=high)
-    factor = step_size * math.sqrt(FF / D)
-    updated = (weight.astype(jnp.float32) - factor * jnp.dot(new_basis, ortho, precision=high)).astype(jnp.bfloat16)
-    full_rows = lax.all_to_all(updated.T, "dp", split_axis=0, concat_axis=1, tiled=True)
-    row_values, row_scales = quantize(full_rows)
-    full_columns = lax.all_to_all(updated, "tensor", split_axis=0, concat_axis=1, tiled=True)
-    column_values, column_scales = quantize(full_columns)
-    return (new_momentum, new_basis, row_values, row_scales, column_values, column_scales)
+    return apply_update(weight, momentum, gradient, wide, inverse, proj)
 
 
 def solution(mesh):

time: 225 us -> 185 us (0.82)
  waiting for transfers between devices: 22.6 us -> 0 us
  Pallas kernels: 154 us -> 175 us
  starting transfers between devices: 16.2 us -> 0 us
  local copies, waits for them, and re-layouts: 19.1 us -> 8.85 us
  matrix products: 6.73 us -> 0 us
  other arithmetic: 4.44 us -> 0 us
    all_to_all x2 -> x0, waiting for transfers between devices: 22.6 us -> none  [the longest x1 14.7 us: on_device(): lax.all_to_all(updated.T, 'dp', split_axis=0, concat_axis=1, tiled=True)]
    pallas_call x1, Pallas kernels: 22.4 us -> 43.5 us  [apply_update(): pl.pallas_call(apply_kernel, out_shape=(shape((rows, columns), f32), shap...]
    all_to_all x2 -> x0, starting transfers between devices: 16.2 us -> none  [the longest x1 10.3 us: on_device(): lax.all_to_all(updated.T, 'dp', split_axis=0, concat_axis=1, tiled=True)]
    dot_general x4 -> x0, matrix products: 6.73 us -> none  [the longest x1 3.82 us: on_device(): jnp.dot(back, ortho, precision=high)]
    all_to_all x2 -> x0, local copies, waits for them, and re-layouts: 3.1 us -> none  [the longest x1 2.13 us: on_device(): lax.all_to_all(updated.T, 'dp', split_axis=0, concat_axis=1, tiled=True)]
    abs x4 -> x0, local copies, waits for them, and re-layouts: 2.74 us -> none  [quantize(): largest = jnp.max(jnp.abs(tiles), axis=2)]
    unnamed x29 -> x22, local copies, waits for them, and re-layouts: 8.9 us -> 8.85 us
  transfers between devices with their start and end apart: 2 -> 0, of which waited for: 2 -> 0; matrix products, arithmetic and copies ran while one was open for 5% -> 0% of each run, Pallas kernels for 0% -> 0%
where the time goes in v2:
time: 185 us; the launch traced here: 184 us
  Pallas kernels  175 us (95%)
  local copies, waits for them, and re-layouts  8.85 us (5%)
    pallas_call x1, Pallas kernels, proj_transposed(): pl.pallas_call(proj_kernel, out_shape=jax.ShapeDtypeStruct((RANK, columns...  50.7 us
    pallas_call x1, Pallas kernels, gram_and_wide(): pl.pallas_call(sums_kernel, out_shape=(jax.ShapeDtypeStruct((RANK, RANK),...  50.1 us
    pallas_call x1, Pallas kernels, apply_update(): pl.pallas_call(apply_kernel, out_shape=(shape((rows, columns), f32), shap...  43.5 us
    pallas_call x1, Pallas kernels, inverse_factor(): pl.pallas_call(cholesky_kernel, out_shape=jax.ShapeDtypeStruct(gram.shape...  30.5 us
    unnamed x22, local copies, waits for them, and re-layouts  8.85 us

profile of v2, /device:TPU:1, one launch (start us, length us, event | category | flops | bytes accessed | tf_op | source)
XLA Modules:
  0.0 184.5 jit_solution(4972606086421567019)
XLA Ops:
  0.6 0.0 copy-start.1
  0.6 1.2 copy-done.1
  1.9 0.0 copy-start.3
  1.9 1.0 copy-done.3
  2.9 0.0 copy-start.7
  2.9 1.0 copy-done.7
  3.9 50.7 %shard_map.91.proj = bf16[512,1152]{1,0:T(8,128)(2,1)S(1)} custom-call(f32[224,1152]{1,0:T(8,128)S(1)} %copy-done.1, bf16[224,1152]{1,0:T(8,128)(2,1)S(1)} %copy-done.3, f32[224,512]{1,0:T(8,128)S(1)} %copy-done.7), custom_call_target="tpu_custom_call" | custom-call | tf_op jit(solution)/shard_map/pallas_call | solution.py:264
  54.6 0.0 copy-start
  54.6 50.1 %shard_map.92 = (f32[512,512]{1,0:T(8,128)S(1)}, f32[224,512]{1,0:T(8,128)S(1)}) custom-call(f32[224,1152]{1,0:T(8,128)S(1)} %copy-done.1, bf16[224,1152]{1,0:T(8,128)(2,1)S(1)} %copy-done.3, bf16[512,1152]{1,0:T(8,128)(2,1)S(1)} %shard_map.91.proj), custom_call_target="tpu_custom_call" | custom-call | tf_op jit(solution)/shard_map/pallas_call | solution.py:431
  104.8 0.0 copy-done
  104.8 0.0 copy-start.2
  104.8 0.0 copy-start.4
  104.8 0.0 copy-start.6
  104.8 30.5 %shard_map.93.inverse = f32[512,512]{1,0:T(8,128)S(1)} custom-call(f32[512,512]{1,0:T(8,128)S(1)} %get-tuple-element.9.gram_ref), custom_call_target="tpu_custom_call" | custom-call | tf_op jit(solution)/shard_map/pallas_call | solution.py:91
  135.4 0.0 copy-start.5
  135.4 1.0 copy-done.5
  136.4 0.0 copy-done.2
  136.4 0.0 copy-done.4
  136.4 0.0 copy-done.6
  136.4 43.5 %shard_map.94 = (f32[224,1152]{1,0:T(8,128)S(1)}, f32[224,512]{1,0:T(8,128)S(1)}, bf16[36,7168]{1,0:T(8,128)(2,1)S(1)}, f32[36,56]{1,0:T(8,128)S(1)}, bf16[14,18...) custom-call(bf16[224,1152]{1,0:T(8,128)(2,1)S(1)} %copy-done.6, f32[224,1152]{1,0:T(8,128)S(1)} %copy-done.2, ...), custom_call_target="tpu_custom_call" | custom-call | tf_op jit(solution)/shard_map/pallas_call | solution.py:625
  179.9 1.0 copy.16
  180.9 0.8 copy.17
  181.7 0.8 copy.18
  182.5 0.6 copy.19
  183.1 0.8 copy.20
  183.9 0.6 copy.21
Async XLA Ops:
  0.6 1.2 copy-start.1
  1.9 1.0 copy-start.3
  2.9 1.0 copy-start.7
  54.6 50.2 %copy-start = (bf16[512,1152]{1,0:T(8,128)(2,1)}, bf16[512,1152]{1,0:T(8,128)(2,1)S(1)}, u32[]{:S(2)}) copy-start(bf16[512,1152]{1,0:T(8,128)(2,1)S(1)} %shard_map.91.proj) | copy-start | bytes 3538948
  104.8 31.6 %copy-start.2 = (f32[224,1152]{1,0:T(8,128)S(1)}, f32[224,1152]{1,0:T(8,128)}, u32[]{:S(2)}) copy-start(f32[224,1152]{1,0:T(8,128)} %momentum.5) | copy-start | bytes 3096580
  104.8 31.6 %copy-start.4 = (bf16[224,1152]{1,0:T(8,128)(2,1)S(1)}, bf16[224,1152]{1,0:T(8,128)(2,1)}, u32[]{:S(2)}) copy-start(bf16[224,1152]{1,0:T(8,128)(2,1)} %gradient.5) | copy-start | bytes 1548292
  104.8 31.5 %copy-start.6 = (bf16[224,1152]{1,0:T(8,128)(2,1)S(1)}, bf16[224,1152]{1,0:T(8,128)(2,1)}, u32[]{:S(2)}) copy-start(bf16[224,1152]{1,0:T(8,128)(2,1)} %weight.1) | copy-start | bytes 1548292
  135.4 1.0 copy-start.5

commit v3 on v2

--- a/solution.py
+++ b/solution.py
@@ -63,9 +63,8 @@
     return own
 
 
-def cholesky_kernel(gram_ref, inv_ref, a_ref, small_ref):
-    a_ref[...] = gram_ref[...]
-    rank = gram_ref.shape[0]
+def factor_and_invert(inv_ref, a_ref, small_ref):
+    rank = a_ref.shape[0]
     row_of = lax.broadcasted_iota(jnp.int32, (rank, rank), 0)
     inv_ref[...] = jnp.where(row_of == lax.broadcasted_iota(jnp.int32, (rank, rank), 1), 1.0, 0.0).astype(jnp.float32)
 
@@ -87,17 +86,6 @@
     lax.fori_loop(0, rank // BLOCK, step, 0)
 
 
-def inverse_factor(gram):
-    return pl.pallas_call(
-        cholesky_kernel,
-        out_shape=jax.ShapeDtypeStruct(gram.shape, jnp.float32),
-        in_specs=[pl.BlockSpec(memory_space=pltpu.VMEM)],
-        out_specs=pl.BlockSpec(memory_space=pltpu.VMEM),
-        scratch_shapes=[pltpu.VMEM(gram.shape, jnp.float32), pltpu.VMEM((BLOCK, BLOCK), jnp.float32)],
-        compiler_params=pltpu.CompilerParams(vmem_limit_bytes=48 << 20),
-    )(gram)
-
-
 D = 7168
 FF = 18432
 TILE = 128
@@ -128,55 +116,58 @@
     return pl.ds(pl.multiple_of(SLAB * (CHIPS * lax.rem(dp, 2) + dp // 2), SLAB), SLAB)
 
 
-def spread_slabs(buffer, dp, tensor, send, recv, pass_send, pass_recv):
+LONG = CHIPS // 2
+
+
+def spread_slabs(slab, dp, tensor, recv, ring_send, cross_send, pass_send, pass_recv):
     core, chip = lax.rem(dp, 2), dp // 2
+    side, z = chip // LONG, lax.rem(chip, LONG)
     other = dp + 1 - 2 * core
-
-    def rows(which):
-        return buffer.at[slab_rows(which), :]
-
-    def copy(step):
-        to = lax.rem(chip + step, CHIPS)
-        return remote(rows(dp), rows(dp), send.at[step], recv.at[chip], 2 * to + core, tensor)
-
-    def arrival(source):
-        return remote(rows(2 * source + core), rows(2 * source + core), send.at[0], recv.at[source], dp, tensor)
-
-    def onward(source):
-        return remote(rows(2 * source + core), rows(2 * source + core), pass_send.at[source], pass_recv.at[source], other, tensor)
-
-    def passed(source):
-        there = rows(2 * source + 1 - core)
-        return remote(there, there, pass_send.at[source], pass_recv.at[source], other, tensor)
-
-    def begin(step, carry):
-        copy(step).start()
-        return carry
-
-    def forward(step, carry):
-        source = lax.rem(chip + CHIPS - step, CHIPS)
-        arrival(source).wait_recv()
-        onward(source).start()
-        return carry
-
-    def finish(step, carry):
-        passed(lax.rem(chip + CHIPS - step, CHIPS)).wait_recv()
-        return carry
-
-    def drain(step, carry):
-        copy(step).wait_send()
-        return carry
-
-    def drain_pass(step, carry):
-        onward(lax.rem(chip + CHIPS - step, CHIPS)).wait_send()
-        return carry
-
-    lax.fori_loop(1, CHIPS, begin, 0)
-    onward(chip).start()
-    lax.fori_loop(1, CHIPS, forward, 0)
-    lax.fori_loop(0, CHIPS, finish, 0)
-    lax.fori_loop(1, CHIPS, drain, 0)
-    lax.fori_loop(0, CHIPS, drain_pass, 0)
+    started = []
+
+    def at(which_side, offset):
+        return LONG * which_side + lax.rem(z + offset + LONG, LONG)
+
+    def mine(source):
+        return slab(2 * source + core)
+
+    def send(source, target, sem):
+        copy = remote(mine(source), mine(source), sem, recv.at[source], 2 * target + core, tensor)
+        copy.start()
+        started.append(copy)
+
+    def hand_over(source):
+        copy = remote(mine(source), mine(source), pass_send.at[source], pass_recv.at[source], other, tensor)
+        copy.start()
+        started.append(copy)
+
+    def arrived(source):
+        remote(mine(source), mine(source), ring_send.at[0], recv.at[source], other, tensor).wait_recv()
+
+    across = at(1 - side, 0)
+    offsets = [4, 3, -3, 2, -2, 1, -1]
+    for offset in offsets:
+        send(chip, at(side, offset), ring_send.at[offset % LONG])
+    send(chip, across, cross_send.at[0])
+    hand_over(chip)
+    for offset in reversed(offsets):
+        source = at(side, offset)
+        arrived(source)
+        send(source, across, cross_send.at[offset % LONG])
+        hand_over(source)
+    for offset in [0] + offsets[::-1]:
+        source = at(1 - side, offset)
+        arrived(source)
+        hand_over(source)
+
+    def passed(step, carry):
+        source = lax.rem(chip + step, CHIPS)
+        there = slab(2 * source + 1 - core)
+        remote(there, there, pass_send.at[source], pass_recv.at[source], other, tensor).wait_recv()
+        return carry
+
+    lax.fori_loop(0, CHIPS, passed, 0)
+    return started
 
 
 def greet_dp(barrier, dp, tensor):
@@ -191,18 +182,32 @@
     pl.semaphore_signal(barrier, inc=1, device_id=(dp + 1 - 2 * core, tensor), device_id_type=MESH)
 
 
-def proj_kernel(momentum, gradient, basis, proj, high, low, basis_high, basis_low, pair_out, pair_in, part, inbox,
-                pair_sems, send, recv, all_send, all_recv, pass_send, pass_recv):
+OWNERS = 5
+TALL = RANK // 8
+WIDE_ROWS, WIDE_COLUMNS = 64, 128
+
+
+def factor_kernel(momentum, gradient, basis, proj, wide, inverse, high, low, basis_high, basis_low, pair_out, pair_in, part, inbox,
+                  gram, work, block, gram_part, gram_inbox, wide_part, wide_inbox, wide_all, pair_sems, send, recv,
+                  tile_send, tile_recv, back_send, back_recv, wide_send, wide_recv, out_send, out_recv, *gather_sems):
+    proj_sems, gram_sems = gather_sems[:len(gather_sems) // 2], gather_sems[len(gather_sems) // 2:]
     dp, tensor = lax.axis_index("dp"), lax.axis_index("tensor")
     core, chip = lax.rem(dp, 2), dp // 2
     other = dp + 1 - 2 * core
     half = RANK // 2
+    rows, columns = momentum.shape
+    width = columns // 3
 
     barrier = pltpu.get_barrier_semaphore()
     greet_dp(barrier, dp, tensor)
 
-    columns = momentum.shape[1]
-    width = columns // 3
+    def greet(step, carry):
+        to = lax.rem(tensor + step, TENSOR)
+        pl.semaphore_signal(barrier, inc=1, device_id=(dp, to), device_id_type=MESH)
+        return carry
+
+    lax.fori_loop(1, TENSOR, greet, 0)
+
     for j in range(3):
         span = pl.ds(j * width, width)
         high[:, span], low[:, span] = halves(momentum[:, span] + gradient[:, span].astype(jnp.float32))
@@ -219,7 +224,7 @@
 
     for j in range(3):
         pair_out[:, pl.ds(j * width, width)] = product((1 - core) * half, j)
-    pl.semaphore_wait(barrier, CHIPS)
+    pl.semaphore_wait(barrier, CHIPS + TENSOR - 1)
     swap = remote(pair_out, pair_in, pair_sems.at[0], pair_sems.at[1], other, tensor)
     swap.start()
     mine = [product(core * half, j) for j in range(3)]
@@ -231,85 +236,43 @@
     def slab(which):
         return part.at[pl.ds(pl.multiple_of(which * SLAB, SLAB), SLAB), :]
 
-    def copy(step):
+    def slab_copy(step):
         to = lax.rem(chip + step, CHIPS)
         return remote(slab(to), inbox.at[chip], send.at[step], recv.at[chip], 2 * to + core, tensor)
 
-    def begin(step, carry):
-        copy(step).start()
-        return carry
-
-    def arrive(step, total):
+    def slab_begin(step, carry):
+        slab_copy(step).start()
+        return carry
+
+    def slab_arrive(step, total):
         source = lax.rem(chip + CHIPS - step, CHIPS)
         remote(inbox.at[source], inbox.at[source], send.at[0], recv.at[source], other, tensor).wait_recv()
         return total + inbox[source].astype(jnp.float32)
 
-    def drain(step, carry):
-        copy(step).wait_send()
-        return carry
-
-    lax.fori_loop(1, CHIPS, begin, 0)
+    def slab_drain(step, carry):
+        slab_copy(step).wait_send()
+        return carry
+
+    lax.fori_loop(1, CHIPS, slab_begin, 0)
     total = part[pl.ds(pl.multiple_of(chip * SLAB, SLAB), SLAB), :].astype(jnp.float32)
-    total = lax.fori_loop(1, CHIPS, arrive, total)
+    total = lax.fori_loop(1, CHIPS, slab_arrive, total)
     proj[slab_rows(dp), :] = total.astype(jnp.bfloat16)
-    spread_slabs(proj, dp, tensor, all_send, all_recv, pass_send, pass_recv)
-    lax.fori_loop(1, CHIPS, drain, 0)
-    swap.wait_send()
-
-
-def proj_transposed(momentum, gradient, basis):
-    rows, columns = momentum.shape
-    half = RANK // 2
-    dma = pltpu.SemaphoreType.DMA
-    return pl.pallas_call(
-        proj_kernel,
-        out_shape=jax.ShapeDtypeStruct((RANK, columns), jnp.bfloat16),
-        in_specs=[VMEM] * 3,
-        out_specs=VMEM,
-        scratch_shapes=[
-            pltpu.VMEM((rows, columns), jnp.bfloat16),
-            pltpu.VMEM((rows, columns), jnp.bfloat16),
-            pltpu.VMEM((RANK, rows), jnp.bfloat16),
-            pltpu.VMEM((RANK, rows), jnp.bfloat16),
-            pltpu.VMEM((half, columns), jnp.float32),
-            pltpu.VMEM((half, columns), jnp.float32),
-            pltpu.VMEM((half, columns), jnp.bfloat16),
-            pltpu.VMEM((CHIPS, SLAB, columns), jnp.bfloat16),
-            dma((2,)), dma((CHIPS,)), dma((CHIPS,)), dma((CHIPS,)), dma((CHIPS,)), dma((CHIPS,)), dma((CHIPS,)),
-        ],
-        compiler_params=pltpu.CompilerParams(collective_id=0, has_side_effects=True, vmem_limit_bytes=48 << 20),
-    )(momentum, gradient, basis)
-
-
-OWNERS = 8
-WIDE_ROWS, WIDE_COLUMNS = 64, 128
-
-
-def sums_kernel(momentum, gradient, proj, gram, wide, gram_part, gram_inbox, wide_part, wide_inbox, wide_all,
-                tile_send, tile_recv, back_send, back_recv, wide_send, wide_recv, out_send, out_recv,
-                all_send, all_recv, pass_send, pass_recv):
-    dp, tensor = lax.axis_index("dp"), lax.axis_index("tensor")
-    rows = momentum.shape[0]
-    barrier = pltpu.get_barrier_semaphore()
-    greet_dp(barrier, dp, tensor)
-
-    def greet(step, carry):
-        to = lax.rem(tensor + step, TENSOR)
-        pl.semaphore_signal(barrier, inc=1, device_id=(dp, to), device_id_type=MESH)
-        return carry
-
-    lax.fori_loop(1, TENSOR, greet, 0)
-
-    gram_part[...] = dot_nt(proj[slab_rows(dp), :], proj[...])
-    pl.semaphore_wait(barrier, CHIPS + TENSOR - 1)
-
-    def tile(ref, first, owner):
-        return ref.at[
-            pl.ds(pl.multiple_of(first + 8 * (owner // 4), 8), 8), pl.ds(pl.multiple_of(128 * lax.rem(owner, 4), 128), 128)
-        ]
+    proj_sends = spread_slabs(lambda which: proj.at[slab_rows(which), :], dp, tensor, *proj_sems)
+
+    def tile_row(which):
+        both = dot_nt(proj[pl.ds(pl.multiple_of(16 * (which // 2), 16), 16), :], proj[...])
+        return jnp.where(lax.rem(which, 2) == 0, both[:8], both[8:])
+
+    upper, lower = tile_row(dp), tile_row(TALL - 1 - dp)
+    column = lambda x, j: x[:, BLOCK * j:BLOCK * (j + 1)]
+    short = dp < TALL // 4
+    gram_part[0] = column(upper, 0)
+    gram_part[1] = jnp.where(short, column(lower, 0), column(upper, 1))
+    for j in range(2, OWNERS):
+        gram_part[j] = jnp.where(short, column(lower, j - 1), column(lower, j - 2))
 
     def tile_copy(owner):
-        return remote(tile(gram_part, 0, owner), gram_inbox.at[tensor], tile_send.at[owner], tile_recv.at[tensor], dp, owner)
+        return remote(gram_part.at[owner], gram_inbox.at[tensor], tile_send.at[owner], tile_recv.at[tensor], dp, owner)
 
     def tile_begin(owner, carry):
         @pl.when(owner != tensor)
@@ -319,32 +282,11 @@
         return carry
 
     lax.fori_loop(0, OWNERS, tile_begin, 0)
-
-    high, low = halves(momentum[...] + gradient[...].astype(jnp.float32))
-    wide_part[:rows, :] = (dot_nt(high, proj[...]) + dot_nt(low, proj[...])).astype(jnp.bfloat16)
-    wide_part[rows:, :] = jnp.zeros((wide_part.shape[0] - rows, RANK), jnp.bfloat16)
-
-    def piece(ref, which):
-        return ref.at[
-            pl.ds(pl.multiple_of(WIDE_ROWS * (which // 4), WIDE_ROWS), WIDE_ROWS),
-            pl.ds(pl.multiple_of(WIDE_COLUMNS * lax.rem(which, 4), WIDE_COLUMNS), WIDE_COLUMNS),
-        ]
-
-    def wide_copy(step):
-        to = lax.rem(tensor + step, TENSOR)
-        return remote(piece(wide_part, to), wide_inbox.at[tensor], wide_send.at[step], wide_recv.at[tensor], dp, to)
-
-    def wide_begin(step, carry):
-        wide_copy(step).start()
-        return carry
-
-    lax.fori_loop(1, TENSOR, wide_begin, 0)
-
-    first = SLAB * (CHIPS * lax.rem(dp, 2) + dp // 2)
+    work[:rows, :] = dot_nt(high[...], proj[...])
 
     def back_copy(step):
         to = lax.rem(tensor + step, TENSOR)
-        here = tile(gram, first, tensor)
+        here = gram.at[dp, tensor]
         return remote(here, here, back_send.at[step], back_recv.at[tensor], dp, to)
 
     @pl.when(tensor < OWNERS)
@@ -359,9 +301,27 @@
             back_copy(step).start()
             return carry
 
-        total = lax.fori_loop(1, TENSOR, arrive, tile(gram_part, 0, tensor)[...])
-        tile(gram, first, tensor)[...] = total
+        gram[dp, tensor] = lax.fori_loop(1, TENSOR, arrive, gram_part[tensor])
         lax.fori_loop(1, TENSOR, back_begin, 0)
+
+    wide_part[:rows, :] = (work[:rows, :] + dot_nt(low[...], proj[...])).astype(jnp.bfloat16)
+    wide_part[rows:, :] = jnp.zeros((wide_part.shape[0] - rows, RANK), jnp.bfloat16)
+
+    def piece(ref, which):
+        return ref.at[
+            pl.ds(pl.multiple_of(WIDE_ROWS * (which // 4), WIDE_ROWS), WIDE_ROWS),
+            pl.ds(pl.multiple_of(WIDE_COLUMNS * lax.rem(which, 4), WIDE_COLUMNS), WIDE_COLUMNS),
+        ]
+
+    def wide_copy(step):
+        to = lax.rem(tensor + step, TENSOR)
+        return remote(piece(wide_part, to), wide_inbox.at[tensor], wide_send.at[step], wide_recv.at[tensor], dp, to)
+
+    def wide_begin(step, carry):
+        wide_copy(step).start()
+        return carry
+
+    lax.fori_loop(1, TENSOR, wide_begin, 0)
 
     def wide_arrive(step, total):
         source = lax.rem(tensor + step, TENSOR)
@@ -381,18 +341,23 @@
     def back_arrive(owner, carry):
         @pl.when(owner != tensor)
         def _():
-            there = tile(gram, first, owner)
+            there = gram.at[dp, owner]
             remote(there, there, back_send.at[0], back_recv.at[owner], dp, tensor).wait_recv()
 
         return carry
 
     lax.fori_loop(0, OWNERS, back_arrive, 0)
-    spread_slabs(gram, dp, tensor, all_send, all_recv, pass_send, pass_recv)
-
+    gram_sends = spread_slabs(lambda which: gram.at[which], dp, tensor, *gram_sems)
+    work[...] = jnp.zeros_like(work)
+    for i in range(DP):
+        places = [(r, j) for r in (i, TALL - 1 - i) for j in range(8 * r // BLOCK + 1)]
+        for j, (r, c) in enumerate(places):
+            work[pl.ds(8 * r, 8), pl.ds(BLOCK * c, BLOCK)] = gram[i, j]
     piece(wide_all, tensor)[...] = lax.fori_loop(
         1, TENSOR, wide_arrive, piece(wide_part, tensor)[...].astype(jnp.float32)
     )
     lax.fori_loop(1, TENSOR, out_begin, 0)
+    factor_and_invert(inverse, work, block)
 
     def out_arrive(step, carry):
         source = lax.rem(tensor + step, TENSOR)
@@ -420,31 +385,53 @@
 
         return carry
 
+    for copy in proj_sends + gram_sends:
+        copy.wait_send()
+    swap.wait_send()
+    lax.fori_loop(1, CHIPS, slab_drain, 0)
     lax.fori_loop(0, OWNERS, tile_drain, 0)
     lax.fori_loop(1, TENSOR, drain, 0)
 
 
-def gram_and_wide(momentum, gradient, proj):
-    rows = momentum.shape[0]
+def factor(momentum, gradient, basis):
+    rows, columns = momentum.shape
+    half = RANK // 2
     padded = TENSOR // 4 * WIDE_ROWS
     dma = pltpu.SemaphoreType.DMA
+    f32, bf16 = jnp.float32, jnp.bfloat16
+    gather = [dma((CHIPS,)), dma((LONG,)), dma((LONG,)), dma((CHIPS,)), dma((CHIPS,))]
     return pl.pallas_call(
-        sums_kernel,
-        out_shape=(jax.ShapeDtypeStruct((RANK, RANK), jnp.float32), jax.ShapeDtypeStruct((rows, RANK), jnp.float32)),
+        factor_kernel,
+        out_shape=(
+            jax.ShapeDtypeStruct((RANK, columns), bf16),
+            jax.ShapeDtypeStruct((rows, RANK), f32),
+            jax.ShapeDtypeStruct((RANK, RANK), f32),
+        ),
         in_specs=[VMEM] * 3,
-        out_specs=(VMEM, VMEM),
+        out_specs=(VMEM,) * 3,
         scratch_shapes=[
-            pltpu.VMEM((SLAB, RANK), jnp.float32),
-            pltpu.VMEM((TENSOR, 8, 128), jnp.float32),
-            pltpu.VMEM((padded, RANK), jnp.bfloat16),
-            pltpu.VMEM((TENSOR, WIDE_ROWS, WIDE_COLUMNS), jnp.bfloat16),
-            pltpu.VMEM((padded, RANK), jnp.float32),
+            pltpu.VMEM((rows, columns), bf16),
+            pltpu.VMEM((rows, columns), bf16),
+            pltpu.VMEM((RANK, rows), bf16),
+            pltpu.VMEM((RANK, rows), bf16),
+            pltpu.VMEM((half, columns), f32),
+            pltpu.VMEM((half, columns), f32),
+            pltpu.VMEM((half, columns), bf16),
+            pltpu.VMEM((CHIPS, SLAB, columns), bf16),
+            pltpu.VMEM((DP, OWNERS, 8, BLOCK), f32),
+            pltpu.VMEM((RANK, RANK), f32),
+            pltpu.VMEM((BLOCK, BLOCK), f32),
+            pltpu.VMEM((OWNERS, 8, BLOCK), f32),
+            pltpu.VMEM((TENSOR, 8, 128), f32),
+            pltpu.VMEM((padded, RANK), bf16),
+            pltpu.VMEM((TENSOR, WIDE_ROWS, WIDE_COLUMNS), bf16),
+            pltpu.VMEM((padded, RANK), f32),
+            dma((2,)), dma((CHIPS,)), dma((CHIPS,)),
             dma((OWNERS,)), dma((TENSOR,)), dma((TENSOR,)), dma((OWNERS,)),
             dma((TENSOR,)), dma((TENSOR,)), dma((TENSOR,)), dma((TENSOR,)),
-            dma((CHIPS,)), dma((CHIPS,)), dma((CHIPS,)), dma((CHIPS,)),
-        ],
-        compiler_params=pltpu.CompilerParams(collective_id=1, has_side_effects=True, vmem_limit_bytes=48 << 20),
-    )(momentum, gradient, proj)
+        ] + gather + gather,
+        compiler_params=pltpu.CompilerParams(collective_id=0, has_side_effects=True, vmem_limit_bytes=48 << 20),
+    )(momentum, gradient, basis)
 
 
 CHUNK = 48
@@ -650,14 +637,12 @@
             pltpu.VMEM((TENSOR, 16, columns), bf16),
             dma((DP,)), dma((DP,)), dma((DP,)), dma((DP,)), dma((TENSOR,)), dma((TENSOR,)),
         ],
-        compiler_params=pltpu.CompilerParams(collective_id=2, has_side_effects=True, vmem_limit_bytes=48 << 20),
+        compiler_params=pltpu.CompilerParams(collective_id=1, has_side_effects=True, vmem_limit_bytes=48 << 20),
     )(weight, momentum, gradient, wide, inverse, proj)
 
 
 def on_device(weight, gradient, momentum, basis):
-    proj = proj_transposed(momentum, gradient, basis)
-    gram, wide = gram_and_wide(momentum, gradient, proj)
-    inverse = inverse_factor(gram)
+    proj, wide, inverse = factor(momentum, gradient, basis)
     return apply_update(weight, momentum, gradient, wide, inverse, proj)
 
 

time: 185 us -> 158 us (0.85)
  Pallas kernels: 175 us -> 148 us
    pallas_call x3 -> x1, Pallas kernels: 131 us -> 108 us  [factor(): pl.pallas_call(factor_kernel, out_shape=(jax.ShapeDtypeStruct((RANK, colu...]
    pallas_call x1, Pallas kernels: 43.5 us -> 40.1 us  [apply_update(): pl.pallas_call(apply_kernel, out_shape=(shape((rows, columns), f32), shap...]
    unnamed x22 -> x18, local copies, waits for them, and re-layouts: 8.85 us -> 9.84 us
where the time goes in v3:
time: 158 us
  Pallas kernels  148 us (94%)
  local copies, waits for them, and re-layouts  9.84 us (6%)
    pallas_call x1, Pallas kernels, factor(): pl.pallas_call(factor_kernel, out_shape=(jax.ShapeDtypeStruct((RANK, colu...  108 us
    pallas_call x1, Pallas kernels, apply_update(): pl.pallas_call(apply_kernel, out_shape=(shape((rows, columns), f32), shap...  40.1 us
    unnamed x18, local copies, waits for them, and re-layouts  9.84 us

profile of v3, /device:TPU:1, one launch (start us, length us, event | category | flops | bytes accessed | tf_op | source)
XLA Modules:
  0.0 158.2 jit_solution(10424906217963889036)
XLA Ops:
  0.6 0.0 copy-start
  0.6 1.2 copy-done
  1.9 0.0 copy-start.1
  1.9 1.0 copy-done.1
  2.9 0.0 copy-start.5
  2.9 1.0 copy-done.5
  3.9 0.0 copy-start.4
  3.9 107.6 %shard_map.91 = (bf16[512,1152]{1,0:T(8,128)(2,1)S(1)}, f32[224,512]{1,0:T(8,128)S(1)}, f32[512,512]{1,0:T(8,128)S(1)}) custom-call(f32[224,1152]{1,0:T(8,128)S(1)} %copy-done, bf16[224,1152]{1,0:T(8,128)(2,1)S(1)} %copy-done.1, f32[224,512]{1,0:T(8,128)S(1)} %copy-done.5), custom_call_target="tpu_custom_call" | custom-call | tf_op jit(solution)/shard_map/pallas_call | solution.py:403
  111.5 0.0 copy-start.2
  111.5 1.0 copy-done.2
  112.5 0.0 copy-start.3
  112.5 1.0 copy-done.3
  113.5 0.0 copy-done.4
  113.5 40.1 %shard_map.92 = (f32[224,1152]{1,0:T(8,128)S(1)}, f32[224,512]{1,0:T(8,128)S(1)}, bf16[36,7168]{1,0:T(8,128)(2,1)S(1)}, f32[36,56]{1,0:T(8,128)S(1)}, bf16[14,18...) custom-call(bf16[224,1152]{1,0:T(8,128)(2,1)S(1)} %copy-done.4, f32[224,1152]{1,0:T(8,128)S(1)} %copy-done, ...), custom_call_target="tpu_custom_call" | custom-call | tf_op jit(solution)/shard_map/pallas_call | solution.py:612
  153.6 1.0 copy.16
  154.6 0.8 copy.17
  155.3 0.8 copy.18
  156.1 0.6 copy.19
  156.7 0.8 copy.20
  157.6 0.6 copy.21
Async XLA Ops:
  0.6 1.2 copy-start
  1.9 1.0 copy-start.1
  2.9 1.0 copy-start.5
  3.9 109.6 %copy-start.4 = (bf16[224,1152]{1,0:T(8,128)(2,1)S(1)}, bf16[224,1152]{1,0:T(8,128)(2,1)}, u32[]{:S(2)}) copy-start(bf16[224,1152]{1,0:T(8,128)(2,1)} %weight.1) | copy-start | bytes 1548292
  111.5 1.0 copy-start.2
  112.5 1.0 copy-start.3

commit v4 on v3

--- a/solution.py
+++ b/solution.py
@@ -1,4 +1,3 @@
-import functools
 import math
 
 import jax
@@ -11,15 +10,14 @@
 RANK = 512
 BLOCK = 128
 STRIP = 8
-HIGHEST = lax.Precision.HIGHEST
-
-
-def dot_nt(a, b, precision=None):
-    return lax.dot_general(a, b, (((1,), (1,)), ((), ())), precision=precision, preferred_element_type=jnp.float32)
-
-
-def dot_nn(a, b, precision=None):
-    return lax.dot_general(a, b, (((1,), (0,)), ((), ())), precision=precision, preferred_element_type=jnp.float32)
+
+
+def dot_nt(a, b):
+    return lax.dot_general(a, b, (((1,), (1,)), ((), ())), preferred_element_type=jnp.float32)
+
+
+def dot_nn(a, b):
+    return lax.dot_general(a, b, (((1,), (0,)), ((), ())), preferred_element_type=jnp.float32)
 
 
 def invert_block(tiles):
@@ -37,14 +35,13 @@
         factor = [[None] * STRIP for _ in range(STRIP)]
         inverse, root = [], []
         for k in range(STRIP):
-            r = lax.rsqrt(small[k][k])
-            root.append(r)
-            inverse.append(r * r)
+            root.append(lax.rsqrt(small[k][k]))
+            inverse.append(1.0 / small[k][k])
             for m in range(k + 1, STRIP):
                 f = small[m][k] * inverse[k]
                 factor[m][k] = f
                 for j in range(k + 1, m + 1):
-                    small[m][j] = small[m][j] - f * small[j][k]
+                    small[m][j] = small[m][j] - (small[m][k] * small[j][k]) * inverse[k]
                 rows[m] = rows[m] - f * rows[k]
                 extra[m] = extra[m] - f * extra[k]
         for i in range(s + 1, count):
@@ -63,27 +60,41 @@
     return own
 
 
-def factor_and_invert(inv_ref, a_ref, small_ref):
+def halves(x):
+    high = x.astype(jnp.bfloat16)
+    return high, (x - high.astype(jnp.float32)).astype(jnp.bfloat16)
+
+
+def split_dot(dot, a, b):
+    a_high, a_low = halves(a)
+    b_high, b_low = halves(b)
+    return dot(a_high, b_high) + (dot(a_high, b_low) + dot(a_low, b_high))
+
+
+def factor_and_invert(inv_ref, a_ref):
     rank = a_ref.shape[0]
-    row_of = lax.broadcasted_iota(jnp.int32, (rank, rank), 0)
-    inv_ref[...] = jnp.where(row_of == lax.broadcasted_iota(jnp.int32, (rank, rank), 1), 1.0, 0.0).astype(jnp.float32)
-
-    def step(b, carry):
-        at = pl.multiple_of(b * BLOCK, BLOCK)
-        tiles = [a_ref[pl.ds(pl.multiple_of(at + STRIP * i, STRIP), STRIP), pl.ds(at, BLOCK)] for i in range(BLOCK // STRIP)]
-        own = invert_block(tiles)
-        for i, tile in enumerate(own):
-            small_ref[pl.ds(STRIP * i, STRIP), :] = tile
-        inverse = small_ref[...]
-        rows = dot_nn(inverse, inv_ref[pl.ds(at, BLOCK), :], HIGHEST)
-        below = lax.broadcasted_iota(jnp.int32, (rank, BLOCK), 0) >= at + BLOCK
-        panel = jnp.where(below, dot_nt(a_ref[:, pl.ds(at, BLOCK)], inverse, HIGHEST), 0.0)
-        inv_ref[pl.ds(at, BLOCK), :] = rows
-        a_ref[...] -= dot_nt(panel, panel, HIGHEST)
-        inv_ref[...] -= dot_nn(panel, rows, HIGHEST)
-        return carry
-
-    lax.fori_loop(0, rank // BLOCK, step, 0)
+    blocks = rank // BLOCK
+    span = lambda b: pl.ds(b * BLOCK, BLOCK)
+    inv_ref[...] = jnp.zeros_like(inv_ref)
+    diagonal = a_ref[span(0), span(0)]
+    for b in range(blocks):
+        inverse = jnp.concatenate(invert_block([diagonal[STRIP * i:STRIP * (i + 1)] for i in range(BLOCK // STRIP)]), axis=0)
+        done, end = pl.ds(0, b * BLOCK), (b + 1) * BLOCK
+        rest = pl.ds(end, rank - end)
+        if b + 1 < blocks:
+            near = split_dot(dot_nt, a_ref[span(b + 1), span(b)], inverse)
+            diagonal = a_ref[span(b + 1), span(b + 1)] - split_dot(dot_nt, near, near)
+        inv_ref[span(b), span(b)] = inverse
+        if b:
+            inv_ref[span(b), done] = split_dot(dot_nn, inverse, inv_ref[span(b), done])
+        if b + 1 < blocks:
+            panel = near
+            if b + 2 < blocks:
+                far = pl.ds(end + BLOCK, rank - end - BLOCK)
+                distant = split_dot(dot_nt, a_ref[far, span(b)], inverse)
+                panel = jnp.concatenate([near, distant], axis=0)
+                a_ref[far, rest] -= split_dot(dot_nt, distant, panel)
+            inv_ref[rest, pl.ds(0, end)] -= split_dot(dot_nn, panel, inv_ref[span(b), pl.ds(0, end)])
 
 
 D = 7168
@@ -99,11 +110,7 @@
 SLAB = RANK // DP
 MESH = pl.DeviceIdType.MESH
 VMEM = pl.BlockSpec(memory_space=pltpu.VMEM)
-
-
-def halves(x):
-    high = x.astype(jnp.bfloat16)
-    return high, (x - high.astype(jnp.float32)).astype(jnp.bfloat16)
+ANY = pl.BlockSpec(memory_space=pl.ANY)
 
 
 def remote(src, dst, send, recv, dp, tensor):
@@ -170,26 +177,25 @@
     return started
 
 
-def greet_dp(barrier, dp, tensor):
-    core, chip = lax.rem(dp, 2), dp // 2
-
-    def greet(step, carry):
-        to = lax.rem(chip + step, CHIPS)
-        pl.semaphore_signal(barrier, inc=1, device_id=(2 * to + core, tensor), device_id_type=MESH)
-        return carry
-
-    lax.fori_loop(1, CHIPS, greet, 0)
-    pl.semaphore_signal(barrier, inc=1, device_id=(dp + 1 - 2 * core, tensor), device_id_type=MESH)
-
-
 OWNERS = 5
 TALL = RANK // 8
 WIDE_ROWS, WIDE_COLUMNS = 64, 128
 
 
-def factor_kernel(momentum, gradient, basis, proj, wide, inverse, high, low, basis_high, basis_low, pair_out, pair_in, part, inbox,
-                  gram, work, block, gram_part, gram_inbox, wide_part, wide_inbox, wide_all, pair_sems, send, recv,
-                  tile_send, tile_recv, back_send, back_recv, wide_send, wide_recv, out_send, out_recv, *gather_sems):
+CHUNK = 48
+ROWS_OUT = FF // TENSOR // DP
+COLUMNS_OUT = D // DP // TENSOR
+TURN = 32
+
+
+def step_kernel(weight_in, momentum_in, gradient_in, basis_in,
+                new_momentum, new_basis, row_values, row_scales, column_values, column_scales,
+                weight, momentum, gradient, basis, high, low, basis_high, basis_low, pair_out, pair_in, part, inbox, proj,
+                gram, work, inverse, gram_part, gram_inbox, wide_part, wide_inbox, wide_all,
+                back_high, fresh_high, fresh_low, ortho_high, ortho_low, square_inbox, update, turned, flipped,
+                row_out, row_in, column_out, column_in, load, pair_send, pair_recv, send, recv,
+                tile_send, tile_recv, back_send, back_recv, wide_send, wide_recv, out_send, out_recv,
+                square_send, square_recv, row_send, row_recv, column_send, column_recv, *gather_sems):
     proj_sems, gram_sems = gather_sems[:len(gather_sems) // 2], gather_sems[len(gather_sems) // 2:]
     dp, tensor = lax.axis_index("dp"), lax.axis_index("tensor")
     core, chip = lax.rem(dp, 2), dp // 2
@@ -198,20 +204,31 @@
     rows, columns = momentum.shape
     width = columns // 3
 
+    loads = [
+        pltpu.make_async_copy(source, target, load.at[i])
+        for i, (source, target) in enumerate(
+            [(basis_in, basis), (gradient_in, gradient), (momentum_in, momentum), (weight_in, weight)]
+        )
+    ]
+    for copy in loads:
+        copy.start()
     barrier = pltpu.get_barrier_semaphore()
-    greet_dp(barrier, dp, tensor)
-
-    def greet(step, carry):
-        to = lax.rem(tensor + step, TENSOR)
-        pl.semaphore_signal(barrier, inc=1, device_id=(dp, to), device_id_type=MESH)
-        return carry
-
-    lax.fori_loop(1, TENSOR, greet, 0)
-
-    for j in range(3):
-        span = pl.ds(j * width, width)
-        high[:, span], low[:, span] = halves(momentum[:, span] + gradient[:, span].astype(jnp.float32))
+
+    def greet_rows(step, carry):
+        pl.semaphore_signal(barrier, inc=1, device_id=(lax.rem(dp + step, DP), tensor), device_id_type=MESH)
+        return carry
+
+    def greet_columns(step, carry):
+        pl.semaphore_signal(barrier, inc=1, device_id=(dp, lax.rem(tensor + step, TENSOR)), device_id_type=MESH)
+        return carry
+
+    lax.fori_loop(1, DP, greet_rows, 0)
+    lax.fori_loop(1, TENSOR, greet_columns, 0)
+
+    loads[0].wait()
     basis_high[...], basis_low[...] = halves(jnp.transpose(basis[...]))
+    loads[1].wait()
+    loads[2].wait()
 
     def product(first, j):
         span = pl.ds(j * width, width)
@@ -222,16 +239,18 @@
             + dot_nn(basis_low[rows, :], high[:, span])
         )
 
-    for j in range(3):
-        pair_out[:, pl.ds(j * width, width)] = product((1 - core) * half, j)
-    pl.semaphore_wait(barrier, CHIPS + TENSOR - 1)
-    swap = remote(pair_out, pair_in, pair_sems.at[0], pair_sems.at[1], other, tensor)
-    swap.start()
-    mine = [product(core * half, j) for j in range(3)]
-    swap.wait_recv()
+    swaps = [remote(pair_out.at[j], pair_in.at[j], pair_send.at[j], pair_recv.at[j], other, tensor) for j in range(3)]
     for j in range(3):
         span = pl.ds(j * width, width)
-        part[:, span] = (mine[j] + pair_in[:, span]).astype(jnp.bfloat16)
+        high[:, span], low[:, span] = halves(momentum[:, span] + gradient[:, span].astype(jnp.float32))
+        pair_out[j] = product((1 - core) * half, j)
+        if j == 0:
+            pl.semaphore_wait(barrier, DP + TENSOR - 2)
+        swaps[j].start()
+    mine = [product(core * half, j) for j in range(3)]
+    for j in range(3):
+        swaps[j].wait_recv()
+        part[:, pl.ds(j * width, width)] = (mine[j] + pair_in[j]).astype(jnp.bfloat16)
 
     def slab(which):
         return part.at[pl.ds(pl.multiple_of(which * SLAB, SLAB), SLAB), :]
@@ -254,6 +273,8 @@
         return carry
 
     lax.fori_loop(1, CHIPS, slab_begin, 0)
+    column_out[...] = jnp.zeros(column_out.shape, jnp.bfloat16)
+    row_out[...] = jnp.zeros(row_out.shape, jnp.bfloat16)
     total = part[pl.ds(pl.multiple_of(chip * SLAB, SLAB), SLAB), :].astype(jnp.float32)
     total = lax.fori_loop(1, CHIPS, slab_arrive, total)
     proj[slab_rows(dp), :] = total.astype(jnp.bfloat16)
@@ -357,7 +378,7 @@
         1, TENSOR, wide_arrive, piece(wide_part, tensor)[...].astype(jnp.float32)
     )
     lax.fori_loop(1, TENSOR, out_begin, 0)
-    factor_and_invert(inverse, work, block)
+    factor_and_invert(inverse, work)
 
     def out_arrive(step, carry):
         source = lax.rem(tensor + step, TENSOR)
@@ -366,109 +387,15 @@
         return carry
 
     lax.fori_loop(1, TENSOR, out_arrive, 0)
-    wide[...] = wide_all[:rows, :]
-
-    def tile_drain(owner, carry):
-        @pl.when(owner != tensor)
-        def _():
-            tile_copy(owner).wait_send()
-
-        return carry
-
-    def drain(step, carry):
-        wide_copy(step).wait_send()
-        out_copy(step).wait_send()
-
-        @pl.when(tensor < OWNERS)
-        def _():
-            back_copy(step).wait_send()
-
-        return carry
-
-    for copy in proj_sends + gram_sends:
-        copy.wait_send()
-    swap.wait_send()
-    lax.fori_loop(1, CHIPS, slab_drain, 0)
-    lax.fori_loop(0, OWNERS, tile_drain, 0)
-    lax.fori_loop(1, TENSOR, drain, 0)
-
-
-def factor(momentum, gradient, basis):
-    rows, columns = momentum.shape
-    half = RANK // 2
-    padded = TENSOR // 4 * WIDE_ROWS
-    dma = pltpu.SemaphoreType.DMA
-    f32, bf16 = jnp.float32, jnp.bfloat16
-    gather = [dma((CHIPS,)), dma((LONG,)), dma((LONG,)), dma((CHIPS,)), dma((CHIPS,))]
-    return pl.pallas_call(
-        factor_kernel,
-        out_shape=(
-            jax.ShapeDtypeStruct((RANK, columns), bf16),
-            jax.ShapeDtypeStruct((rows, RANK), f32),
-            jax.ShapeDtypeStruct((RANK, RANK), f32),
-        ),
-        in_specs=[VMEM] * 3,
-        out_specs=(VMEM,) * 3,
-        scratch_shapes=[
-            pltpu.VMEM((rows, columns), bf16),
-            pltpu.VMEM((rows, columns), bf16),
-            pltpu.VMEM((RANK, rows), bf16),
-            pltpu.VMEM((RANK, rows), bf16),
-            pltpu.VMEM((half, columns), f32),
-            pltpu.VMEM((half, columns), f32),
-            pltpu.VMEM((half, columns), bf16),
-            pltpu.VMEM((CHIPS, SLAB, columns), bf16),
-            pltpu.VMEM((DP, OWNERS, 8, BLOCK), f32),
-            pltpu.VMEM((RANK, RANK), f32),
-            pltpu.VMEM((BLOCK, BLOCK), f32),
-            pltpu.VMEM((OWNERS, 8, BLOCK), f32),
-            pltpu.VMEM((TENSOR, 8, 128), f32),
-            pltpu.VMEM((padded, RANK), bf16),
-            pltpu.VMEM((TENSOR, WIDE_ROWS, WIDE_COLUMNS), bf16),
-            pltpu.VMEM((padded, RANK), f32),
-            dma((2,)), dma((CHIPS,)), dma((CHIPS,)),
-            dma((OWNERS,)), dma((TENSOR,)), dma((TENSOR,)), dma((OWNERS,)),
-            dma((TENSOR,)), dma((TENSOR,)), dma((TENSOR,)), dma((TENSOR,)),
-        ] + gather + gather,
-        compiler_params=pltpu.CompilerParams(collective_id=0, has_side_effects=True, vmem_limit_bytes=48 << 20),
-    )(momentum, gradient, basis)
-
-
-CHUNK = 48
-ROWS_OUT = FF // TENSOR // DP
-COLUMNS_OUT = D // DP // TENSOR
-TURN = 32
-
-
-def apply_kernel(weight, momentum, gradient, wide, inverse, proj,
-                 new_momentum, new_basis, row_values, row_scales, column_values, column_scales,
-                 back_high, basis_high, basis_low, ortho_high, ortho_low, square_inbox, update, turned, flipped, row_out, row_in, column_out, column_in,
-                 square_send, square_recv, row_send, row_recv, column_send, column_recv):
-    dp, tensor = lax.axis_index("dp"), lax.axis_index("tensor")
-    rows, columns = weight.shape
-    width = columns // 3
-    barrier = pltpu.get_barrier_semaphore()
-
-    def greet_rows(step, carry):
-        pl.semaphore_signal(barrier, inc=1, device_id=(lax.rem(dp + step, DP), tensor), device_id_type=MESH)
-        return carry
-
-    def greet_columns(step, carry):
-        pl.semaphore_signal(barrier, inc=1, device_id=(dp, lax.rem(tensor + step, TENSOR)), device_id_type=MESH)
-        return carry
-
-    lax.fori_loop(1, DP, greet_rows, 0)
-    lax.fori_loop(1, TENSOR, greet_columns, 0)
 
     inverse_high, inverse_low = halves(inverse[...])
-    wide_high, wide_low = halves(wide[...])
+    wide_high, wide_low = halves(wide_all[:rows, :])
     back = dot_nt(wide_high, inverse_high) + dot_nt(wide_low, inverse_high) + dot_nt(wide_high, inverse_low)
     squares = jnp.sum(jnp.sum((back * back).reshape(rows // 8, 8, RANK), axis=0), axis=0, keepdims=True)
     lanes = RANK // 4
     square_inbox[dp] = jnp.concatenate(
         [squares[:, j * lanes:(j + 1) * lanes] for j in range(4)] + [jnp.zeros((4, lanes), jnp.float32)], axis=0
     )
-    pl.semaphore_wait(barrier, DP + TENSOR - 2)
 
     def square_copy(step):
         here = square_inbox.at[dp]
@@ -498,16 +425,18 @@
     colsq = jnp.concatenate([total[j:j + 1, :] for j in range(4)], axis=1)
     fresh = back / jnp.sqrt(colsq + epsilon)
     new_basis[...] = fresh
-    basis_high[...], basis_low[...] = halves(fresh)
+    fresh_high[...], fresh_low[...] = halves(fresh)
+
+    loads[3].wait()
 
     factor = step_size * math.sqrt(FF / D)
     shift = lax.rem(3 * dp, 4)
     for j in range(3):
         span = pl.ds(j * width, width)
         product = (
-            dot_nn(basis_high[...], ortho_high[:, span])
-            + dot_nn(basis_low[...], ortho_high[:, span])
-            + dot_nn(basis_high[...], ortho_low[:, span])
+            dot_nn(fresh_high[...], ortho_high[:, span])
+            + dot_nn(fresh_low[...], ortho_high[:, span])
+            + dot_nn(fresh_high[...], ortho_low[:, span])
         )
         update[:, span] = weight[:, span].astype(jnp.float32) - factor * product
 
@@ -527,8 +456,6 @@
         column_copy(step).start()
         return carry
 
-    column_out[...] = jnp.zeros(column_out.shape, jnp.bfloat16)
-    row_out[...] = jnp.zeros(row_out.shape, jnp.bfloat16)
     pieces = rows // TURN
     for i in range(pieces + 1):
         to = pl.ds(pl.multiple_of(TURN * lax.rem(i + shift, pieces + 1), TURN), TURN)
@@ -549,47 +476,79 @@
         product = dot_nn(back_high[...], ortho_high[:, span])
         new_momentum[:, span] = momentum[:, span] + gradient[:, span].astype(jnp.float32) - (1.0 - decay_rate) * product
 
-    def column_arrive(step, carry):
-        source = lax.rem(tensor + step, TENSOR)
-        there = column_in.at[source]
-        remote(there, there, column_send.at[0], column_recv.at[source], dp, tensor).wait_recv()
-        return carry
-
-    def row_arrive(step, carry):
-        source = lax.rem(dp + step, DP)
-        there = row_in.at[source]
-        remote(there, there, row_send.at[0], row_recv.at[source], dp, tensor).wait_recv()
-        return carry
-
     def scaled(tile):
         largest = jnp.max(jnp.abs(tile), axis=1, keepdims=True)
         return (tile * (1.0 / (largest + epsilon))).astype(jnp.bfloat16), largest
 
-    lax.fori_loop(1, TENSOR, column_arrive, 0)
-    count = columns // TILE
-    lane_of = lax.broadcasted_iota(jnp.int32, (16, 256), 1)
-    scales = jnp.zeros((16, 256), jnp.float32)
-    for source in range(TENSOR):
-        for j in range(count):
+    def column_quantize(step, scales):
+        source = lax.rem(tensor + step, TENSOR)
+        there = column_in.at[source]
+
+        @pl.when(step > 0)
+        def _():
+            remote(there, there, column_send.at[0], column_recv.at[source], dp, tensor).wait_recv()
+
+        lane_of = lax.broadcasted_iota(jnp.int32, scales.shape, 1)
+        for j in range(columns // TILE):
             values, largest = scaled(column_in[source, :, pl.ds(TILE * j, TILE)].astype(jnp.float32))
-            column_values[:, pl.ds(columns * source + TILE * j, TILE)] = values[:COLUMNS_OUT]
-            scales = jnp.where(lane_of == count * source + j, largest, scales)
+            column_values[:, pl.ds(pl.multiple_of(columns * source + TILE * j, TILE), TILE)] = values[:COLUMNS_OUT]
+            scales = jnp.where(lane_of == columns // TILE * source + j, largest, scales)
+        return scales
+
+    scales = lax.fori_loop(0, TENSOR, column_quantize, jnp.zeros((16, 2 * TILE), jnp.float32))
     column_scales[...] = scales[:COLUMNS_OUT, :FF // TILE]
 
-    lax.fori_loop(1, DP, row_arrive, 0)
-    lane_of = lax.broadcasted_iota(jnp.int32, (CHUNK, TILE), 1)
-    scales = jnp.zeros((CHUNK, TILE), jnp.float32)
-    for tile in range(D // TILE):
-        source = TILE * tile // rows
-        part = lambda which: row_in[which, :, pl.ds(TILE * ((tile - rows * which // TILE) % 2), TILE)].astype(jnp.float32)
-        block = part(source)
-        bound = rows * (source + 1) - TILE * tile
-        if bound < TILE:
-            block = jnp.where(lane_of < bound, block, part(source + 1))
-        values, largest = scaled(block)
-        row_values[:, pl.ds(TILE * tile, TILE)] = values[:ROWS_OUT]
-        scales = jnp.where(lane_of == tile, largest, scales)
+    def row_quantize(step, scales):
+        group = lax.rem(dp // 4 + (1 - 2 * lax.rem(step, 2)) * ((step + 1) // 2) + DP // 4, DP // 4)
+        first = pl.multiple_of(4 * rows * group, TILE)
+        lane_of = lax.broadcasted_iota(jnp.int32, scales.shape, 1)
+        for i in range(4):
+            source = 4 * group + i
+
+            @pl.when(source != dp)
+            def _():
+                there = row_in.at[source]
+                remote(there, there, row_send.at[0], row_recv.at[source], dp, tensor).wait_recv()
+
+        for tile in range(4 * rows // TILE):
+            which = TILE * tile // rows
+            take = lambda i: row_in[4 * group + i, :, pl.ds(TILE * ((tile - rows * i // TILE) % 2), TILE)].astype(jnp.float32)
+            block = take(which)
+            bound = rows * (which + 1) - TILE * tile
+            if bound < TILE:
+                block = jnp.where(lane_of < bound, block, take(which + 1))
+            values, largest = scaled(block)
+            row_values[:, pl.ds(pl.multiple_of(first + TILE * tile, TILE), TILE)] = values[:ROWS_OUT]
+            scales = jnp.where(lane_of == 4 * rows // TILE * group + tile, largest, scales)
+        return scales
+
+    scales = lax.fori_loop(0, DP // 4, row_quantize, jnp.zeros((CHUNK, TILE), jnp.float32))
     row_scales[...] = scales[:ROWS_OUT, :D // TILE]
+
+    def tile_drain(owner, carry):
+        @pl.when(owner != tensor)
+        def _():
+            tile_copy(owner).wait_send()
+
+        return carry
+
+    def drain(step, carry):
+        wide_copy(step).wait_send()
+        out_copy(step).wait_send()
+
+        @pl.when(tensor < OWNERS)
+        def _():
+            back_copy(step).wait_send()
+
+        return carry
+
+    for copy in proj_sends + gram_sends:
+        copy.wait_send()
+    for copy in swaps:
+        copy.wait_send()
+    lax.fori_loop(1, CHIPS, slab_drain, 0)
+    lax.fori_loop(0, OWNERS, tile_drain, 0)
+    lax.fori_loop(1, TENSOR, drain, 0)
 
     def square_drain(step, carry):
         square_copy(step).wait_send()
@@ -604,13 +563,16 @@
     lax.fori_loop(1, TENSOR, column_drain, 0)
 
 
-def apply_update(weight, momentum, gradient, wide, inverse, proj):
+def step(weight, momentum, gradient, basis):
     rows, columns = weight.shape
+    half = RANK // 2
+    padded = TENSOR // 4 * WIDE_ROWS
     dma = pltpu.SemaphoreType.DMA
     f32, bf16 = jnp.float32, jnp.bfloat16
-    shape = jax.ShapeDtypeStruct
+    shape, vmem = jax.ShapeDtypeStruct, pltpu.VMEM
+    gather = [dma((CHIPS,)), dma((LONG,)), dma((LONG,)), dma((CHIPS,)), dma((CHIPS,))]
     return pl.pallas_call(
-        apply_kernel,
+        step_kernel,
         out_shape=(
             shape((rows, columns), f32),
             shape((rows, RANK), f32),
@@ -619,31 +581,54 @@
             shape((COLUMNS_OUT, FF), bf16),
             shape((COLUMNS_OUT, FF // TILE), f32),
         ),
-        in_specs=[VMEM] * 6,
+        in_specs=[ANY] * 4,
         out_specs=(VMEM,) * 6,
         scratch_shapes=[
-            pltpu.VMEM((rows, RANK), bf16),
-            pltpu.VMEM((rows, RANK), bf16),
-            pltpu.VMEM((rows, RANK), bf16),
-            pltpu.VMEM((RANK, columns), bf16),
-            pltpu.VMEM((RANK, columns), bf16),
-            pltpu.VMEM((DP, 8, RANK // 4), f32),
-            pltpu.VMEM((rows, columns), f32),
-            pltpu.VMEM((rows + TURN, columns), f32),
-            pltpu.VMEM((columns, rows + TURN), f32),
-            pltpu.VMEM((DP, CHUNK, rows + TURN), bf16),
-            pltpu.VMEM((DP, CHUNK, rows + TURN), bf16),
-            pltpu.VMEM((TENSOR, 16, columns), bf16),
-            pltpu.VMEM((TENSOR, 16, columns), bf16),
+            vmem((rows, columns), bf16),
+            vmem((rows, columns), f32),
+            vmem((rows, columns), bf16),
+            vmem((rows, RANK), f32),
+            vmem((rows, columns), bf16),
+            vmem((rows, columns), bf16),
+            vmem((RANK, rows), bf16),
+            vmem((RANK, rows), bf16),
+            vmem((3, half, columns // 3), f32),
+            vmem((3, half, columns // 3), f32),
+            vmem((half, columns), bf16),
+            vmem((CHIPS, SLAB, columns), bf16),
+            vmem((RANK, columns), bf16),
+            vmem((DP, OWNERS, 8, BLOCK), f32),
+            vmem((RANK, RANK), f32),
+            vmem((RANK, RANK), f32),
+            vmem((OWNERS, 8, BLOCK), f32),
+            vmem((TENSOR, 8, BLOCK), f32),
+            vmem((padded, RANK), bf16),
+            vmem((TENSOR, WIDE_ROWS, WIDE_COLUMNS), bf16),
+            vmem((padded, RANK), f32),
+            vmem((rows, RANK), bf16),
+            vmem((rows, RANK), bf16),
+            vmem((rows, RANK), bf16),
+            vmem((RANK, columns), bf16),
+            vmem((RANK, columns), bf16),
+            vmem((DP, 8, RANK // 4), f32),
+            vmem((rows, columns), f32),
+            vmem((rows + TURN, columns), f32),
+            vmem((columns, rows + TURN), f32),
+            vmem((DP, CHUNK, rows + TURN), bf16),
+            vmem((DP, CHUNK, rows + TURN), bf16),
+            vmem((TENSOR, 16, columns), bf16),
+            vmem((TENSOR, 16, columns), bf16),
+            dma((4,)), dma((3,)), dma((3,)), dma((CHIPS,)), dma((CHIPS,)),
+            dma((OWNERS,)), dma((TENSOR,)), dma((TENSOR,)), dma((OWNERS,)),
+            dma((TENSOR,)), dma((TENSOR,)), dma((TENSOR,)), dma((TENSOR,)),
             dma((DP,)), dma((DP,)), dma((DP,)), dma((DP,)), dma((TENSOR,)), dma((TENSOR,)),
-        ],
-        compiler_params=pltpu.CompilerParams(collective_id=1, has_side_effects=True, vmem_limit_bytes=48 << 20),
-    )(weight, momentum, gradient, wide, inverse, proj)
+        ] + gather + gather,
+        compiler_params=pltpu.CompilerParams(collective_id=0, has_side_effects=True, vmem_limit_bytes=56 << 20),
+    )(weight, momentum, gradient, basis)
 
 
 def on_device(weight, gradient, momentum, basis):
-    proj, wide, inverse = factor(momentum, gradient, basis)
-    return apply_update(weight, momentum, gradient, wide, inverse, proj)
+    return step(weight, momentum, gradient, basis)
 
 
 def solution(mesh):

time: 158 us -> 137 us (0.87)
  Pallas kernels: 148 us -> 129 us
  local copies, waits for them, and re-layouts: 9.84 us -> 6.37 us
    pallas_call x2 -> x1, Pallas kernels: 148 us -> 129 us  [step(): pl.pallas_call(step_kernel, out_shape=(shape((rows, columns), f32), shape...]
    unnamed x18 -> x16, local copies, waits for them, and re-layouts: 9.84 us -> 6.37 us
where the time goes in v4:
time: 137 us; the launch traced here: 136 us
  Pallas kernels  129 us (94%)
  local copies, waits for them, and re-layouts  6.37 us (5%)
    pallas_call x1, Pallas kernels, step(): pl.pallas_call(step_kernel, out_shape=(shape((rows, columns), f32), shape...  129 us
    unnamed x16, local copies, waits for them, and re-layouts  6.37 us

profile of v4, /device:TPU:1, one launch (start us, length us, event | category | flops | bytes accessed | tf_op | source)
XLA Modules:
  0.0 136.5 jit_solution(18089438622107577766)
XLA Ops:
  0.6 129.4 %shard_map.91 = (f32[224,1152]{1,0:T(8,128)}, f32[224,512]{1,0:T(8,128)}, bf16[36,7168]{1,0:T(8,128)(2,1)}, f32[36,56]{1,0:T(8,128)}, bf16[14,18432]{1,0:T(8,128)(2,1)}, /*index=5*/f32[14,144]{1,0:T(8,128)}) custom-call(bf16[224,1152]{1,0:T(8,128)(2,1)} %weight_in.1, f32[224,1152]{1,0:T(8,128)} %momentum_in.1, bf16[224,1152]{1,0:T(8,128)(2,1)} %gradient_in.1, ...), custom_call_target="tpu_custom_call" | custom-call | tf_op jit(solution)/shard_map/pallas_call | solution.py:574
  130.1 0.0 copy-start.2
  130.1 2.3 %copy.16 = f32[224,1152]{1,0:T(8,128)} copy(f32[224,1152]{1,0:T(8,128)} %get-tuple-element.12) | data formatting | bytes 2064384
  132.4 0.0 copy-done.2
  132.4 0.0 copy-start.1
  132.4 0.8 copy.17
  133.2 0.5 copy-done.1
  133.6 0.0 copy-start.3
  133.6 0.0 copy-start
  133.6 0.8 copy.18
  134.4 0.0 copy-done.3
  134.4 0.6 copy.19
  135.0 0.0 copy-done
  135.0 0.0 copy-start.4
  135.0 0.8 copy.20
  135.9 0.0 copy-done.4
  135.9 0.6 copy.21
Async XLA Ops:
  130.1 2.3 %copy-start.2 = (f32[224,512]{1,0:T(8,128)S(1)}, f32[224,512]{1,0:T(8,128)}, u32[]{:S(2)}) copy-start(f32[224,512]{1,0:T(8,128)} %get-tuple-element.13) | copy-start | bytes 1376260
  132.4 1.2 copy-start.1
  133.6 0.8 copy-start.3
  133.6 1.4 %copy-start = (bf16[14,18432]{1,0:T(8,128)(2,1)S(1)}, bf16[14,18432]{1,0:T(8,128)(2,1)}, u32[]{:S(2)}) copy-start(bf16[14,18432]{1,0:T(8,128)(2,1)} %get-tuple-element.16) | copy-start | bytes 1548292
  135.0 0.8 copy-start.4

commit v5 on v4

--- a/solution.py
+++ b/solution.py
@@ -627,8 +627,29 @@
     )(weight, momentum, gradient, basis)
 
 
+def settle_kernel(*refs):
+    sems, count = refs[-1], len(refs) // 2
+    copies = [pltpu.make_async_copy(refs[i], refs[count + i], sems.at[i]) for i in range(count)]
+    for copy in copies:
+        copy.start()
+    for copy in copies:
+        copy.wait()
+
+
+def settle(arrays):
+    count = len(arrays)
+    return pl.pallas_call(
+        settle_kernel,
+        out_shape=tuple(jax.ShapeDtypeStruct(x.shape, x.dtype) for x in arrays),
+        in_specs=[VMEM] * count,
+        out_specs=(ANY,) * count,
+        scratch_shapes=[pltpu.SemaphoreType.DMA((count,))],
+        compiler_params=pltpu.CompilerParams(vmem_limit_bytes=16 << 20),
+    )(*arrays)
+
+
 def on_device(weight, gradient, momentum, basis):
-    return step(weight, momentum, gradient, basis)
+    return settle(step(weight, momentum, gradient, basis))
 
 
 def solution(mesh):

time: 137 us -> 138 us (level)
  Pallas kernels: 129 us -> 131 us
    pallas_call x0 -> x1, Pallas kernels: none -> 1.55 us  [settle(): pl.pallas_call(settle_kernel, out_shape=tuple((jax.ShapeDtypeStruct(x.sha...]
    unnamed x16 -> x12, local copies, waits for them, and re-layouts: 6.37 us -> 5.8 us
where the time goes in v5:
time: 138 us
  Pallas kernels  131 us (95%)
  local copies, waits for them, and re-layouts  5.8 us (4%)
    pallas_call x1, Pallas kernels, step(): pl.pallas_call(step_kernel, out_shape=(shape((rows, columns), f32), shape...  129 us
    unnamed x12, local copies, waits for them, and re-layouts  5.8 us

profile of v5, /device:TPU:1, one launch (start us, length us, event | category | flops | bytes accessed | tf_op | source)
XLA Modules:
  0.0 137.7 jit_solution(16905044532454656584)
XLA Ops:
  0.6 129.5 %shard_map.91 = (f32[224,1152]{1,0:T(8,128)}, f32[224,512]{1,0:T(8,128)}, bf16[36,7168]{1,0:T(8,128)(2,1)}, f32[36,56]{1,0:T(8,128)}, bf16[14,18432]{1,0:T(8,128)(2,1)}, /*index=5*/f32[14,144]{1,0:T(8,128)}) custom-call(bf16[224,1152]{1,0:T(8,128)(2,1)} %weight_in.1, f32[224,1152]{1,0:T(8,128)} %momentum_in.1, bf16[224,1152]{1,0:T(8,128)(2,1)} %gradient_in.1, ...), custom_call_target="tpu_custom_call" | custom-call | tf_op jit(solution)/shard_map/pallas_call | solution.py:574
  130.1 0.0 copy-start
  130.1 1.2 copy-done
  131.3 0.0 copy-start.1
  131.3 1.1 copy-done.1
  132.4 0.0 copy-start.2
  132.4 1.1 copy-done.2
  133.5 0.0 copy-start.3
  133.5 1.0 copy-done.3
  134.5 0.0 copy-start.4
  134.5 0.7 copy-done.4
  135.2 0.0 copy-start.5
  135.2 0.7 copy-done.5
  135.9 1.6 %shard_map.92 = (f32[224,1152]{1,0:T(8,128)}, f32[224,512]{1,0:T(8,128)}, bf16[36,7168]{1,0:T(8,128)(2,1)}, f32[36,56]{1,0:T(8,128)}, bf16[14,18432]{1,0:T(8,128)(2,1)}, /*index=5*/f32[14,144]{1,0:T(8,128)}) custom-call(f32[224,1152]{1,0:T(8,128)S(1)} %copy-done, f32[224,512]{1,0:T(8,128)S(1)} %copy-done.3, bf16[36,7168]{1,0:T(8,128)(2,1)S(1)} %copy-done.2, ...), custom_call_target="tpu_custom_call" | custom-call | tf_op jit(solution)/shard_map/pallas_call | solution.py:641
Async XLA Ops:
  130.1 1.2 copy-start
  131.3 1.1 copy-start.1
  132.4 1.1 copy-start.2
  133.5 1.0 copy-start.3
  134.5 0.7 copy-start.4
  135.2 0.7 copy-start.5
